TPU v7x, 32 devices: a whole 2x2x4 slice. The times are simulated.
32 devices in a mesh: dp: 8 (over y, x, core), mp: 4 (over z).
Axes of the slice: x: 2, y: 2, z: 4, core: 2. Of those that a mesh axis runs over, the one named last changes fastest.
Arguments:
- tokens: bfloat16 [24576, 768], P(('dp', 'mp')), may hold values from -6 to 6
- grad_out: bfloat16 [24576, 768], P(('dp', 'mp')), may hold values from -6 to 6
- pass_len: int32 [24, 4], P('dp'), may hold values from 100 to 200, as said below
- labels: int32 [96], P('dp'), may hold values from 0 to 95, each once
- w_query: bfloat16 [768, 768], P(None, 'mp'), may hold values from -0.21875 to 0.21875
- w_key: bfloat16 [768, 768], P(None, 'mp'), may hold values from -0.21875 to 0.21875
- w_value: bfloat16 [768, 768], P(None, 'mp'), may hold values from -0.21875 to 0.21875
- b_query: float32 [768], P('mp'), may hold values from -1 to 1
- b_value: float32 [768], P('mp'), may hold values from -1 to 1
- w_out: bfloat16 [768, 768], P('mp'), may hold values from -1.5 to 1.5
- b_out: float32 [768], replicated, may hold values from -1 to 1
- ln1_gain: float32 [768], replicated, may hold values from 0.5 to 1.5
- ln1_shift: float32 [768], replicated, may hold values from -1 to 1
- w_in: bfloat16 [768, 3072], P(None, 'mp'), may hold values from -0.21875 to 0.21875
- b_in: float32 [3072], P('mp'), may hold values from -1 to 1
- w_back: bfloat16 [3072, 768], P('mp'), may hold values from -0.15625 to 0.15625
- b_back: float32 [768], replicated, may hold values from -1 to 1
- ln2_gain: float32 [768], replicated, may hold values from 0.5 to 1.5
- ln2_shift: float32 [768], replicated, may hold values from -1 to 1
Outputs:
- mixed: bfloat16 [24576, 768], P(('dp', 'mp'))
- query_losses: float32 [96], P('dp')
- d_tokens: float32 [24576, 768], P(('dp', 'mp'))
- d_w_query: float32 [768, 768], P(None, 'mp')
- d_w_key: float32 [768, 768], P(None, 'mp')
- d_w_value: float32 [768, 768], P(None, 'mp')
- d_b_query: float32 [768], P('mp')
- d_b_value: float32 [768], P('mp')
- d_w_out: float32 [768, 768], P('mp')
- d_b_out: float32 [768], P('mp')
- d_ln1_gain: float32 [768], P('mp')
- d_ln1_shift: float32 [768], P('mp')
- d_w_in: float32 [768, 3072], P(None, 'mp')
- d_b_in: float32 [3072], P('mp')
- d_w_back: float32 [3072, 768], P('mp')
- d_b_back: float32 [768], P('mp')
- d_ln2_gain: float32 [768], P('mp')
- d_ln2_shift: float32 [768], P('mp')
Inputs may be any that keep to these rules, and one draw needn't show every extreme that they name: `pass_len`: each passage length lies in the stated range; the passages of a row follow its 4 queries of 32 tokens and the rest of the row is padding; row 0 holds a passage of exactly 200 tokens.
All inputs are finite; a program needn't handle non-finite values.
Results may differ from a plain program's by a relative error of at most 0.015.
The roundings to bfloat16 on the way count: a program that leaves them out, or rounds other values in their place, can miss the bound.
Values may be sent and summed in bfloat16 or wider, within the bound.
No kernel may reach another device: no remote copies, remote signals or barrier semaphores. Data moves between devices by JAX's collectives and lax.ppermute only.
A program may use at most 128 MiB of HBM per device.

v0:
```python
import functools
import math

import jax
import jax.numpy as jnp
from jax import lax
from jax.experimental import pallas as pl
from jax.experimental.pallas import tpu as pltpu
from jax.sharding import PartitionSpec as P

HEAD = 64
ROW_LEN = 1024
PAIRS = 4
QLEN = 32
TILE = 128
QUERIES = 64
QUAD = 4 * HEAD
ALIGN = 32
BLOCKS = (1, 2, 3, 4, 5, 7, 10)

epsilon = 1e-12
masked_score = -1e30
highest = lax.Precision.HIGHEST
f32 = jnp.float32
bf16 = jnp.bfloat16
NT = (((1,), (1,)), ((), ()))
TN = (((0,), (0,)), ((), ()))
NN = (((1,), (0,)), ((), ()))


def mm(a, b, dims=NN):
    return lax.dot_general(a, b, dims, preferred_element_type=f32)


def bounds_kernel(halo, own, start_ref, pass_ref, tiles_ref, low_ref, high_ref):
    start = start_ref[0]
    count = low_ref.shape[1]
    rows = pass_ref.shape[0]
    last = rows * ROW_LEN
    cuts = []
    for row in range(rows):
        cuts += [jnp.int32(row * ROW_LEN + j * QLEN) for j in range(PAIRS + 1)]
        for j in range(PAIRS):
            cuts.append(cuts[-1] + pass_ref[row, j])

    def low_of(place):
        low = jnp.full_like(place, start)
        for cut in cuts:
            low = jnp.where(cut <= place, cut, low)
        return jnp.clip(jnp.where(place >= last, last, low) - start, 0, count)

    def high_of(place):
        high = jnp.full_like(place, last)
        for cut in reversed(cuts):
            high = jnp.where(cut > place, cut, high)
        return jnp.clip(jnp.where(place >= last, start + count, high) - start, 0, count)

    place = start + lax.broadcasted_iota(jnp.int32, (1, count), 1)
    low_ref[...] = low_of(place)
    high_ref[...] = high_of(place)
    for tile in range(count // QUERIES):
        at = tile * QUERIES
        first = low_of(start + at)
        after_last = high_of(start + at + QUERIES - 1)
        low = first // ALIGN * ALIGN
        blocks = (after_last - low + TILE - 1) // TILE
        tiles_ref[0, tile] = low
        tiles_ref[1, tile] = blocks
        if at < halo:
            blocks = jnp.where(after_last > halo, blocks, 0)
        if at >= halo + own:
            blocks = jnp.where(first < halo + own, blocks, 0)
        tiles_ref[2, tile] = blocks


def segment_bounds(pass_len, start, halo, own):
    count = own + 2 * halo
    smem = pl.BlockSpec(memory_space=pltpu.SMEM)
    vmem = pl.BlockSpec(memory_space=pltpu.VMEM)
    line = jax.ShapeDtypeStruct((1, count), jnp.int32)
    return pl.pallas_call(
        functools.partial(bounds_kernel, halo, own),
        out_shape=(jax.ShapeDtypeStruct((3, count // QUERIES), jnp.int32), line, line),
        in_specs=[smem, smem],
        out_specs=(smem, vmem, vmem),
        compiler_params=pltpu.CompilerParams(vmem_limit_bytes=8 * 2**20),
        name="bounds",
    )(start.reshape(1), pass_len)


def cls_places(pass_len):
    lens = [pass_len[:, j] for j in range(PAIRS)]
    starts = [jnp.full_like(lens[0], j * QLEN) for j in range(PAIRS)]
    at = jnp.full_like(lens[0], PAIRS * QLEN)
    for j in range(PAIRS):
        starts.append(at)
        at = at + lens[j]
    return jnp.stack(starts, axis=1)


def by_span(blocks, count, act):
    least = 0
    for size in BLOCKS:
        if size * TILE > count:
            break

        @pl.when((blocks > least) & (blocks <= size))
        def _(size=size):
            act(size * TILE)

        least = size


def head_of(shape):
    return lax.broadcasted_iota(jnp.int32, shape, 1) // HEAD


def split_heads(block):
    head = head_of(block.shape)
    zero = jnp.zeros_like(block)
    return jnp.concatenate([jnp.where(head == h, block, zero) for h in range(4)], axis=0)


def join_heads(stacked):
    rows = stacked.shape[0] // 4
    head = head_of((rows, stacked.shape[1]))
    out = stacked[:rows]
    for h in range(1, 4):
        out = jnp.where(head == h, stacked[h * rows : (h + 1) * rows], out)
    return out


def four_times(ref, row):
    line = ref[:, pl.ds(pl.multiple_of(row // TILE * TILE, TILE), TILE)]
    turned = jnp.concatenate([line[:, QUERIES:], line[:, :QUERIES]], axis=1)
    lane = lax.broadcasted_iota(jnp.int32, line.shape, 1)
    odd = row % TILE >= QUERIES
    both = jnp.where((lane < QUERIES) != odd, line, turned)
    return jnp.concatenate([both, both], axis=1)


def write_bias(bias_ref, lo_ref, hi_ref, row, first, span):
    place = lax.broadcasted_iota(jnp.int32, (span, QUAD), 0) + first
    inside = (place >= four_times(lo_ref, row)) & (place < four_times(hi_ref, row))
    bias_ref[:span] = jnp.where(inside, 0.0, masked_score)


def head_weights(scores, bias):
    scores = [score + bias for score in scores]
    tops = [jnp.max(score, axis=0, keepdims=True) for score in scores]
    raised = [jnp.exp(score - top) for score, top in zip(scores, tops)]
    inverses = [1.0 / jnp.sum(value, axis=0, keepdims=True) for value in raised]
    return [value * inverse for value, inverse in zip(raised, inverses)]


def forward_kernel(halo, start, tiles_ref, lo_ref, hi_ref, q_ref, k_ref, v_ref, out_ref, bias_ref):
    count = k_ref.shape[0]
    quads = [pl.ds(i * QUAD, QUAD) for i in range(q_ref.shape[1] // QUAD)]

    def tile_step(tile, carry):
        here = tile + (start + halo) // QUERIES
        blocks = tiles_ref[1, here]

        def act(span):
            first = jnp.minimum(tiles_ref[0, here], count - span)
            keys = pl.ds(pl.multiple_of(first, ALIGN), span)
            to = pl.ds(pl.multiple_of(tile * QUERIES, QUERIES), QUERIES)
            row = pl.multiple_of(tile * QUERIES + start + halo, QUERIES)
            write_bias(bias_ref, lo_ref, hi_ref, row, first, span)
            rows = pl.ds(row, QUERIES)
            scores = [mm(k_ref[keys, lanes], split_heads(q_ref[rows, lanes]), NT) for lanes in quads]
            weights = [value.astype(bf16) for value in head_weights(scores, bias_ref[:span])]
            for lanes, value in zip(quads, weights):
                out_ref[to, lanes] = join_heads(mm(value, v_ref[keys, lanes], TN)).astype(bf16)

        by_span(blocks, count, act)
        return carry

    lax.fori_loop(0, out_ref.shape[0] // QUERIES, tile_step, 0)


def lasting(micros):
    return pl.CostEstimate(flops=int(micros * 2e7), bytes_accessed=int(micros * 7e4), transcendentals=0)


def attention(kernel, arrays, outs, scratch, micros, name, mib):
    smem = pl.BlockSpec(memory_space=pltpu.SMEM)
    vmem = pl.BlockSpec(memory_space=pltpu.VMEM)
    return pl.pallas_call(
        kernel,
        out_shape=tuple(jax.ShapeDtypeStruct(shape, dtype) for shape, dtype in outs),
        in_specs=[smem] + [vmem] * (len(arrays) - 1),
        out_specs=(vmem,) * len(outs),
        scratch_shapes=[pltpu.VMEM(shape, dtype) for shape, dtype in scratch],
        compiler_params=pltpu.CompilerParams(vmem_limit_bytes=mib * 2**20),
        cost_estimate=lasting(micros),
        name=name,
    )(*arrays)


def attend_forward(bounds, queries, keys, values, halo, part, parts):
    count, width = keys.shape
    rows = (count - 2 * halo) // parts
    (context,) = attention(
        functools.partial(forward_kernel, halo, part * rows), (*bounds, queries, keys, values),
        [((rows, width), bf16)], [((count, QUAD), f32)], 7, "attend_forward", 30,
    )
    return context


def backward_kernel(halo, start, carried, tiles_ref, lo_ref, hi_ref, q_ref, k_ref, v_ref, g_ref, *refs):
    count = k_ref.shape[0]
    own = count - 2 * halo
    if carried:
        dk_in, dv_in, dq_ref, dk_ref, dv_ref, bias_ref, dk_sum, dv_sum = refs
        dk_sum[...] = dk_in[...]
        dv_sum[...] = dv_in[...]
    else:
        dq_ref, dk_sum, dv_sum, bias_ref = refs
        dk_sum[...] = jnp.zeros_like(dk_sum)
        dv_sum[...] = jnp.zeros_like(dv_sum)
    quads = [pl.ds(i * QUAD, QUAD) for i in range(q_ref.shape[1] // QUAD)]
    low = max(start, halo)

    def tile_step(tile, carry):
        blocks = tiles_ref[2, tile]
        mine = (tile >= halo // QUERIES) & (tile < (halo + own) // QUERIES)

        def act(span):
            first = jnp.minimum(tiles_ref[0, tile], count - span)
            keys = pl.ds(pl.multiple_of(first, ALIGN), span)
            row = pl.multiple_of(tile * QUERIES, QUERIES)
            rows = pl.ds(row, QUERIES)
            write_bias(bias_ref, lo_ref, hi_ref, row, first, span)
            q4 = [split_heads(q_ref[rows, lanes]) for lanes in quads]
            scores = [mm(k_ref[keys, lanes], q, NT) for q, lanes in zip(q4, quads)]
            g4 = [split_heads(g_ref[rows, lanes]) for lanes in quads]
            slopes = [mm(v_ref[keys, lanes], g, NT) for g, lanes in zip(g4, quads)]
            weights = head_weights(scores, bias_ref[:span])
            inner = [jnp.sum(w * s, axis=0, keepdims=True) for w, s in zip(weights, slopes)]
            grads = [(w * (s - i)).astype(bf16) for w, s, i in zip(weights, slopes, inner)]
            for w, g, lanes in zip(weights, g4, quads):
                dv_sum[keys, lanes] += mm(w.astype(bf16), g)
            for d, q, lanes in zip(grads, q4, quads):
                dk_sum[keys, lanes] += mm(d, q)

            @pl.when(mine)
            def _():
                to = pl.ds(pl.multiple_of(row - low, QUERIES), QUERIES)
                for d, lanes in zip(grads, quads):
                    grad = join_heads(mm(d, k_ref[keys, lanes], TN)).astype(bf16)
                    dq_ref[to, lanes] = grad * jnp.asarray(1.0 / math.sqrt(HEAD), bf16)

        by_span(blocks, count, act)
        return carry

    tiles = count // QUERIES // 2
    lax.fori_loop(start // QUERIES, start // QUERIES + tiles, tile_step, 0)
    if carried:
        dk_ref[...] = dk_sum[pl.ds(halo, own), :].astype(bf16)
        dv_ref[...] = dv_sum[pl.ds(halo, own), :].astype(bf16)


def attend_backward(bounds, queries, keys, values, grads, halo, sums):
    count, width = keys.shape
    own = count - 2 * halo
    window = ((count, width), f32)
    outs = [((own // 2, width), bf16)]
    if sums:
        outs, scratch = outs + [((own, width), bf16)] * 2, [((count, QUAD), f32), window, window]
    else:
        outs, scratch = outs + [window, window], [((count, QUAD), f32)]
    return attention(
        functools.partial(backward_kernel, halo, count // 2 if sums else 0, bool(sums)),
        (*bounds, queries, keys, values, grads, *sums), outs, scratch, 16, "attend_backward", 48,
    )


SMEM = pl.BlockSpec(memory_space=pltpu.SMEM)
VMEM = pl.BlockSpec(memory_space=pltpu.VMEM)
PLANE = 8


def local(kernel, place, arrays, outs, scratch, micros, name, mib=20):
    return pl.pallas_call(
        kernel,
        out_shape=tuple(jax.ShapeDtypeStruct(shape, dtype) for shape, dtype in outs),
        in_specs=[SMEM] + [VMEM] * len(arrays),
        out_specs=(VMEM,) * len(outs),
        scratch_shapes=[pltpu.VMEM(shape, dtype) for shape, dtype in scratch],
        compiler_params=pltpu.CompilerParams(vmem_limit_bytes=mib * 2**20),
        cost_estimate=lasting(micros),
        name=name,
    )(place, *arrays)


def own_heads_kernel(place_ref, q_ref, k_ref, v_ref, out_ref, rows_ref):
    place = place_ref[0]
    eighths = q_ref.shape[0] // PLANE
    slabs = q_ref.shape[0] // 8
    for i, ref in enumerate((q_ref, k_ref, v_ref)):
        rows_ref[pl.ds(i * slabs, slabs)] = ref[...].astype(f32).reshape(slabs, 8, -1)
    heads = 3 * eighths // 8
    for j in range(PLANE):
        held = [rows_ref[h * PLANE + (place ^ j)] for h in range(heads)]
        out_ref[j] = jnp.concatenate(held, axis=0).astype(bf16)


def own_units_kernel(place_ref, o_ref, i_ref, b_ref, out_ref, in_ref, back_ref, rows_ref, units_ref):
    place = place_ref[0]
    rows = in_ref.shape[1]
    heads = out_ref.shape[1] // 8
    rows_ref[...] = o_ref[...].astype(f32).reshape(rows_ref.shape)
    units_ref[...] = i_ref[...].astype(f32).T.reshape(units_ref.shape)
    for j in range(PLANE):
        held = [rows_ref[h * PLANE + (place ^ j)] for h in range(heads)]
        out_ref[j] = jnp.concatenate(held, axis=0).astype(bf16)
        in_ref[j] = units_ref[place ^ j].astype(bf16)
        back_ref[j] = b_ref[pl.ds(pl.multiple_of((place ^ j) * rows, rows), rows), :]


def by_eighth(refs):
    first, second = [], []
    for j in range(PLANE):
        far, y, x = j // 4, j // 2 % 2, j % 2
        first.append(refs[4].at[y, x] if far else refs[y].at[x])
        second.append(refs[4].at[2 + x, y] if far else refs[2 + x].at[y])
    return first, second


def eighth_rows(halves, j, member, start, count):
    first, second = halves[0][j], halves[1][j]
    middle = first.shape[1]
    pieces = []
    if start < middle:
        pieces.append(first[member, pl.ds(start, min(count, middle - start)), :])
    if start + count > middle:
        at = max(start, middle)
        pieces.append(second[member, pl.ds(at - middle, start + count - at), :])
    return pieces


def stage_eighths(own_ref, halves, member, start, stage_ref):
    for j in range(PLANE):
        if own_ref is not None and member == 0:
            stage_ref[j] = own_ref[j].astype(f32)
            continue
        at = 0
        of = member if own_ref is None else member - 1
        for piece in eighth_rows(halves, j, of, start, stage_ref.shape[1]):
            stage_ref[j, pl.ds(at, piece.shape[0]), :] = piece.astype(f32)
            at += piece.shape[0]


def head_block(stage_ref, head):
    return jnp.concatenate([stage_ref[j, pl.ds(head * 8, 8), :] for j in range(PLANE)], axis=0)


def project_kernel(
    place_ref, left_ref, tokens_ref, right_ref, own_ref, *refs
):
    halves, refs = by_eighth(refs[:5]), refs[5:]
    bias_ref, q_ref, k_ref, v_ref, w_ref, x_ref, stage_ref = refs
    ways = halves[0][0].shape[0] + 1
    heads = own_ref.shape[1] // 24
    halo = left_ref.shape[0]
    own = tokens_ref.shape[0]
    width = tokens_ref.shape[1]
    inner = heads * HEAD
    x_ref[:halo] = left_ref[...]
    x_ref[pl.ds(halo, own)] = tokens_ref[...]
    x_ref[pl.ds(halo + own, halo)] = right_ref[...]
    for member in range(ways):
        stage_eighths(own_ref, halves, member, 0, stage_ref)
        for kind in range(3):
            blocks = [head_block(stage_ref, kind * heads + h) for h in range(heads)]
            at = kind * width + member * inner
            w_ref[pl.ds(at, inner)] = jnp.concatenate(blocks, axis=0).astype(bf16)

    def step(i, carry):
        rows = pl.ds(pl.multiple_of(i * 256, 256), 256)
        x = x_ref[rows, :]
        q = mm(x, w_ref[:width], NT) + bias_ref[0:1]
        q_ref[rows, :] = (q * (1.0 / math.sqrt(HEAD))).astype(bf16)
        k_ref[rows, :] = mm(x, w_ref[pl.ds(width, width)], NT).astype(bf16)
        v_ref[rows, :] = (mm(x, w_ref[pl.ds(2 * width, width)], NT) + bias_ref[1:2]).astype(bf16)
        return carry

    lax.fori_loop(0, x_ref.shape[0] // 256, step, 0)


def join_units(own_ref, halves, out_ref):
    rows = own_ref.shape[1]
    ways = halves[0][0].shape[0] + 1
    for j in range(PLANE):
        out_ref[pl.ds(j * ways * rows, rows), :] = own_ref[j]
        for member in range(1, ways):
            at = (j * ways + member) * rows
            for piece in eighth_rows(halves, j, member - 1, 0, rows):
                out_ref[pl.ds(at, piece.shape[0]), :] = piece
                at += piece.shape[0]


def join_units_kernel(place_ref, own_ref, *refs):
    join_units(own_ref, by_eighth(refs[:5]), refs[5])


def join_in_out_kernel(place_ref, own_ref, own_out_ref, *refs):
    halves = by_eighth(refs[:5])
    in_ref, out_ref, stage_ref = refs[5:]
    join_units(own_ref, halves, in_ref)
    heads = own_out_ref.shape[1] // 8
    for member in range(halves[0][0].shape[0] + 1):
        stage_eighths(own_out_ref, halves, member, own_ref.shape[1], stage_ref)
        for h in range(heads):
            block = head_block(stage_ref, h)
            out_ref[pl.ds((member * heads + h) * HEAD, HEAD), :] = block.astype(bf16)


def split_digits(values):
    digits = []
    for _ in range(3):
        digits.append(values.astype(bf16))
        values = values - digits[-1].astype(f32)
    return digits


def biases_kernel(place_ref, along_ref, in_ref, q_ref, v_ref, heads_ref, units_ref, line_ref):
    place = place_ref[0]
    ways = along_ref.shape[0] + 1
    inner = q_ref.shape[1]
    rows = in_ref.shape[1] // PLANE
    first = along_ref.shape[1] - 8
    others = along_ref[:, first:, :].astype(f32)
    digits = split_digits(jnp.concatenate([q_ref[...], v_ref[...]], axis=1))
    digits = [digit.astype(f32) for digit in digits]
    for member in range(ways - 1):
        digits.append(others[member, 3:6, : 2 * inner])
    digits = jnp.concatenate(digits, axis=0).astype(bf16)
    lane = lax.broadcasted_iota(jnp.int32, (2 * inner, 2 * inner), 0)
    to = lax.broadcasted_iota(jnp.int32, (2 * inner, 2 * inner), 1)
    chosen = jnp.where((lane ^ (place << 3)) == to, 1.0, 0.0).astype(bf16)
    moved = mm(digits, chosen)
    sums = [moved[3 * m : 3 * m + 1] + moved[3 * m + 1 : 3 * m + 2] + moved[3 * m + 2 : 3 * m + 3] for m in range(ways)]
    heads_ref[0:1] = jnp.concatenate([value[:, :inner] for value in sums], axis=1)
    heads_ref[1:2] = jnp.concatenate([value[:, inner:] for value in sums], axis=1)
    for member in range(ways):
        if member == 0:
            value = in_ref[...]
        else:
            three = others[member - 1]
            value = three[0:1] + three[1:2] + three[2:3]
        for p in range(PLANE):
            line_ref[member * PLANE + p, 0:1, :rows] = value[:, p * rows : (p + 1) * rows]
    held = [
        line_ref[member * PLANE + (place ^ j), 0:1, :rows] for j in range(PLANE) for member in range(ways)
    ]
    units_ref[...] = jnp.concatenate(held, axis=1)


def vectors_kernel(place_ref, *refs):
    stat_refs, (units_ref, out_ref, line_ref) = refs[:6], refs[6:]
    place, own = place_ref[0], place_ref[1]
    ways, _, width = out_ref.shape
    inner = width // ways
    rows = units_ref.shape[1] // PLANE // ways
    for j in range(PLANE):
        for member in range(ways):
            at = j * ways + member
            line_ref[at, 0:1, :rows] = units_ref[:, at * rows : (at + 1) * rows]
    stats = jnp.concatenate([ref[...] for ref in stat_refs], axis=0)
    parts = [stats[:, i * inner : (i + 1) * inner] for i in range(ways)]
    for member in range(ways):
        held = [line_ref[(place ^ p) * ways + member, 0:1, :rows] for p in range(PLANE)]
        mine = parts[0]
        for i in range(1, ways):
            mine = jnp.where((own ^ member) == i, parts[i], mine)
        norms = jnp.concatenate([mine[i : i + 1] for i in range(6)], axis=1)
        norms = jnp.concatenate([norms, jnp.zeros((1, 2 * inner), f32)], axis=1)
        lines = [jnp.concatenate(held, axis=1), norms[:, :width], norms[:, width:]]
        out_ref[member] = jnp.concatenate([*lines, jnp.zeros((5, width), f32)], axis=0)


def put_heads(ways, heads, sum_ref, kind, first_head, block):
    for i in range(block.shape[0] // HEAD):
        member, h = divmod(first_head + i, heads)
        for j in range(PLANE):
            part = block[i * HEAD + j * 8 : i * HEAD + j * 8 + 8]
            sum_ref[j * ways + member, pl.ds((kind * heads + h) * 8, 8), :] = part


def part_pieces(sum_ref, keep_ref, send_ref):
    half = keep_ref.shape[0]
    for i in range(half):
        keep_ref[i] = sum_ref[i].astype(bf16)
        send_ref[i] = sum_ref[half + i].astype(bf16)


def out_grads_kernel(ways, place_ref, context_ref, first_ref, keep_ref, send_ref, sum_ref):
    width = first_ref.shape[1]
    heads = width // ways // HEAD
    sum_ref[:, heads * 8 :, :] = jnp.zeros((PLANE * ways, 8, width), f32)
    put_heads(ways, heads, sum_ref, 0, 0, mm(context_ref[...], first_ref[...], TN))
    part_pieces(sum_ref, keep_ref, send_ref)


def piece_grads_kernel(
    place_ref, dq_first_ref, dq_second_ref, dk_ref, dv_ref, tokens_ref, vectors_ref, keep_ref, send_ref, sum_ref
):
    place = place_ref[0]
    ways = vectors_ref.shape[0]
    width = tokens_ref.shape[1]
    inner = width // ways
    heads = inner // HEAD
    half = dq_first_ref.shape[0]
    block = mm(dq_first_ref[...], tokens_ref[:half], TN) + mm(dq_second_ref[...], tokens_ref[half:], TN)
    put_heads(ways, heads, sum_ref, 0, 0, block)
    put_heads(ways, heads, sum_ref, 1, 0, mm(dk_ref[...], tokens_ref[...], TN))
    put_heads(ways, heads, sum_ref, 2, 0, mm(dv_ref[...], tokens_ref[...], TN))
    lane = lax.broadcasted_iota(jnp.int32, (width, width), 0)
    to = lax.broadcasted_iota(jnp.int32, (width, width), 1)
    member = sum((lane >= i * inner).astype(jnp.int32) for i in range(1, ways))
    within = lane - member * inner
    spot = within ^ (place << 3)
    row = lax.broadcasted_iota(jnp.int32, (8, width), 0)
    column = lax.broadcasted_iota(jnp.int32, (8, width), 1)
    of = sum((column >= i * inner).astype(jnp.int32) for i in range(1, ways))
    ones = jnp.ones((8, tokens_ref.shape[0]), bf16)
    lines = jnp.zeros((8, width), f32)
    sums_of = (
        mm(ones[:, :half], dq_first_ref[...]) + mm(ones[:, :half], dq_second_ref[...]),
        mm(ones, dv_ref[...]),
    )
    for sums, first in zip(sums_of, (width - 2 * inner, width - inner)):
        sums = jnp.where(of == row, sums, 0.0)
        chosen = jnp.where(spot + first == to, 1.0, 0.0).astype(bf16)
        lines = lines + mm(sums.astype(bf16), chosen)
    below = 3 * heads * 8
    for i in range(ways):
        block = vectors_ref[i] + jnp.where(row == 2, lines[i : i + 1], 0.0)
        for j in range(PLANE):
            sum_ref[j * ways + i, pl.ds(below, 8), :] = block
    part_pieces(sum_ref, keep_ref, send_ref)


def gather_heads(place, rows_ref, first, out_ref):
    held = []
    for h in range(out_ref.shape[0] // HEAD):
        for p in range(PLANE):
            held.append(rows_ref[place ^ p, pl.ds(first + h * 8, 8), :])
    out_ref[...] = jnp.concatenate(held, axis=0)


def finish_heads_kernel(place_ref, *refs):
    q_ref, k_ref, v_ref, rows_ref = refs[5:]
    stage_eighths(None, by_eighth(refs[:5]), 0, 0, rows_ref)
    for kind, ref in enumerate((q_ref, k_ref, v_ref)):
        gather_heads(place_ref[0], rows_ref, kind * ref.shape[0] // PLANE, ref)


def finish_units_kernel(place_ref, *refs):
    back_ref, in_ref, out_ref, rows_ref, turned_ref = refs[5:]
    place = place_ref[0]
    rows = back_ref.shape[0] // PLANE
    stage_eighths(None, by_eighth(refs[:5]), 0, 0, rows_ref)
    for p in range(PLANE):
        back_ref[pl.ds(p * rows, rows), :] = rows_ref[place ^ p, :rows, :]
        turned_ref[pl.ds(p * rows, rows), :] = rows_ref[place ^ p, pl.ds(rows, rows), :]
    in_ref[...] = turned_ref[...].T
    gather_heads(place, rows_ref, 2 * rows, out_ref)


def norm_parts(values):
    center = values - jnp.mean(values, axis=-1, keepdims=True)
    spread = jnp.mean(center * center, axis=-1, keepdims=True)
    return center, lax.rsqrt(spread + epsilon)


def norm_pull(grad, unit, inverse, gain):
    scaled = grad * gain
    mean = jnp.mean(scaled, axis=-1, keepdims=True)
    along = jnp.mean(scaled * unit, axis=-1, keepdims=True)
    return inverse * (scaled - mean - unit * along)


def gelu_both(before):
    half = 0.5 * (1.0 + lax.erf(before * math.sqrt(0.5)))
    bell = jnp.exp(-0.5 * before * before) * (1.0 / math.sqrt(2.0 * math.pi))
    return before * half, half + before * bell


def partner(values, step):
    ways = lax.axis_size("mp")
    return lax.ppermute(values, "mp", [(i, i ^ step) for i in range(ways)])


def halo_rows(values, halo):
    ways = lax.axis_size("mp")
    before = lax.ppermute(values[-halo:], "mp", [(i, i + 1) for i in range(ways - 1)])
    after = lax.ppermute(values[:halo], "mp", [(i + 1, i) for i in range(ways - 1)])
    return before, after


def group_tables(table):
    ways = lax.axis_size("mp")
    data_ways = lax.axis_size("dp")
    total = table
    for step in range(1, ways):
        total = total + partner(table, step)
    held = total[None]
    data_index = lax.axis_index("dp")
    level = 1
    while level < data_ways:
        other = lax.ppermute(held, "dp", [(i, i ^ level) for i in range(data_ways)])
        first = (data_index & level) == 0
        held = jnp.where(
            first, jnp.concatenate([held, other]), jnp.concatenate([other, held])
        )
        level *= 2
    return held


CORE, NEAR_X, NEAR_Y = 1, 2, 4


def swap(values, bit):
    ways = lax.axis_size("dp")
    return lax.ppermute(values, "dp", [(i, i ^ bit) for i in range(ways)])


def along(piece):
    return [partner(piece, step) for step in range(1, lax.axis_size("mp"))]


def bit_step(held, level, *gates):
    order = sorted(held)
    other = after(partner(jnp.stack([held[i] for i in order]), level), gates)
    return held | {i | level: other[at] for at, i in enumerate(order)}


def others_of(held):
    return jnp.stack([held[i] for i in sorted(held)[1:]])


def first_step(values, *gates):
    middle = values.shape[1] // 2
    first, second = values[:, :middle], values[:, middle:]
    arrived = after((swap(first, NEAR_X), swap(second, NEAR_Y)), gates)
    return [jnp.stack([first, arrived[0]]), jnp.stack([second, arrived[1]])]


def second_step(pairs, *gates):
    first, second = pairs
    arrived = after((swap(first, NEAR_Y), swap(second, NEAR_X)), gates)
    return [first, arrived[0], second, arrived[1]]


def core_step(held):
    return [*held, swap(jnp.stack(held), CORE)]


def after(value, *others):
    return lax.optimization_barrier((value, others))[0]


def add(first, second):
    return (first.astype(f32) + second.astype(f32)).astype(bf16)


def first_sum_step(sums):
    half = sums.shape[2] // 2
    first, second = sums[:, :, :half], sums[:, :, half:]
    return [(first[0], swap(first[1], NEAR_Y)), (second[:, 0], swap(second[:, 1], NEAR_X))]


def second_sum_step(halves):
    first, second = (add(*half) for half in halves)
    return [(first[0], swap(first[1], NEAR_X)), (second[0], swap(second[1], NEAR_Y))]


def over_groups(total):
    level = PLANE
    while level < lax.axis_size("dp"):
        total = total + swap(total, level)
        level *= 2
    return total


def sum_along(parts):
    total = parts[0].astype(f32)
    for step in range(1, len(parts)):
        total = total + partner(parts[step], step).astype(f32)
    return over_groups(total)


def shards(
    tokens, grad_out, pass_len, labels, w_query, w_key, w_value, b_query, b_value, w_out, b_out,
    ln1_gain, ln1_shift, w_in, b_in, w_back, b_back, ln2_gain, ln2_shift,
):
    ways = lax.axis_size("mp")
    data_ways = lax.axis_size("dp")
    mp_index = lax.axis_index("mp")
    data_index = lax.axis_index("dp")
    own_rows, width = tokens.shape
    rows_here = pass_len.shape[0]
    inner = w_query.shape[1]
    units = w_in.shape[1]
    halo = ROW_LEN // 4
    count = own_rows + 2 * halo
    scale = 1.0 / math.sqrt(HEAD)
    temper = 2.0 / math.sqrt(width)

    piece_rows = units // PLANE
    heads = inner // HEAD
    part = inner // PLANE
    place = jnp.stack([(data_index & CORE) << 2 | (data_index % PLANE) >> 1, mp_index])
    (qkv_own,) = local(
        own_heads_kernel, place, (w_query.T, w_key.T, w_value.T), [((PLANE, 3 * part, width), bf16)],
        [((3 * heads * PLANE, 8, width), f32)], 4, "own_heads",
    )
    biases = jnp.concatenate([b_in, b_query, b_value])
    digits, rest = [], biases
    for _ in range(3):
        digits.append(lax.reduce_precision(rest, 8, 7))
        rest = rest - digits[-1]
    digits = jnp.stack(digits)
    lines = jnp.concatenate(
        [digits[:, :units], jnp.pad(digits[:, units:], ((0, 0), (0, width - 2 * inner)))]
    )
    lines = jnp.pad(lines, ((0, 2), (0, 0))).astype(bf16)
    qkv_along = along(jnp.concatenate([qkv_own[0], lines]))
    tokens_before, tokens_after = halo_rows(tokens, halo)
    w_out, w_in, w_back, place = lax.optimization_barrier((w_out, w_in, w_back, place, qkv_own))[:4]
    out_own, in_own, back_own = local(
        own_units_kernel, place, (w_out, w_in, w_back),
        [((PLANE, part, width), bf16), ((PLANE, piece_rows, width), bf16), ((PLANE, piece_rows, width), bf16)],
        [((heads * PLANE, 8, width), f32), ((PLANE, piece_rows, width), f32)], 5, "own_units",
    )
    in_piece = jnp.concatenate([in_own[0], out_own[0], jnp.zeros((8, width), bf16), back_own[0]])
    in_piece = after(in_piece, qkv_along)
    qkv_along = jnp.stack(qkv_along)
    qkv_pairs = first_step(qkv_along)
    in_held = {0: in_piece}
    level = ways // 2
    while level > 1:
        in_held = bit_step(in_held, level)
        level //= 2
    in_held = after(in_held, qkv_pairs)
    qkv_held = second_step(after(qkv_pairs, tokens_before, tokens_after, in_held))
    in_along = others_of(bit_step(in_held, 1))
    bias_heads, bias_in = local(
        biases_kernel, place, (after(qkv_along, qkv_pairs), b_in[None], b_query[None], b_value[None]),
        [((2, width), f32), ((1, ways * units), f32)], [((ways * PLANE, 8, 128), f32)], 2, "biases",
    )
    start = after(mp_index * own_rows - halo, qkv_pairs)
    bounds = segment_bounds(pass_len, start, halo, own_rows)
    qkv_parts = core_step(after(qkv_held, in_along, bias_heads, bounds))
    in_start = after(in_along, qkv_parts)
    in_rows = piece_rows + part + 8

    tokens_before = after(tokens_before, in_along)
    qkv = (tokens_before, tokens, tokens_after, qkv_own, *qkv_parts, bias_heads)
    queries, keys, values, qkv_all = local(
        project_kernel, place, qkv, [((count, width), bf16)] * 3 + [((3 * width, width), bf16)],
        [((count, width), bf16), ((PLANE, 3 * part, width), f32)], 10, "project", 32,
    )
    in_pairs = first_step(in_start[:, :in_rows], queries)
    context = [attend_forward(bounds, after(queries, in_pairs), keys, values, halo, 0, 2)]
    in_held = second_step(in_pairs, context[0])
    back_start = after(in_start[:, in_rows:], in_held)
    in_parts = core_step(in_held)
    late_queries = after(queries, in_held, back_start, context[0])
    context.append(attend_forward(bounds, late_queries, keys, values, halo, 1, 2))
    context = jnp.concatenate(context)
    in_own = after(in_own, context)
    in_all, out_all = local(
        join_in_out_kernel, place, (in_own, out_own, *in_parts),
        [((ways * units, width), bf16), ((width, width), bf16)],
        [((PLANE, part, width), f32)], 5, "join_in_out",
    )
    attended = mm(context, out_all)
    back_held = second_step(first_step(back_start, context), attended)
    back_parts = core_step(back_held)
    (back_all,) = local(
        join_units_kernel, place, (back_own, *back_parts),
        [((ways * units, width), bf16)], [], 4, "join_back",
    )
    first_sum = tokens.astype(f32) + attended + b_out
    center_one, inverse_one = norm_parts(first_sum)
    unit_one = center_one * inverse_one
    hidden = unit_one * ln1_gain + ln1_shift
    hidden_low = after(hidden.astype(bf16), back_held)

    active, slope = gelu_both(mm(hidden_low, in_all, NT) + bias_in)
    active, slope = lax.optimization_barrier((active.astype(bf16), slope.astype(bf16)))
    second_sum = hidden + mm(active, back_all) + b_back
    center_two, inverse_two = norm_parts(second_sum)
    unit_two = center_two * inverse_two
    mixed = (unit_two * ln2_gain + ln2_shift).astype(bf16)

    query_count = PAIRS * rows_here
    places = cls_places(pass_len) + (jnp.arange(rows_here, dtype=jnp.int32) * ROW_LEN)[:, None]
    table_places = jnp.concatenate([places[:, :PAIRS].reshape(-1), places[:, PAIRS:].reshape(-1)])
    table_places = table_places - mp_index * own_rows
    picker = table_places[:, None] == jnp.arange(own_rows, dtype=jnp.int32)[None, :]
    table = mm(picker.astype(bf16), mixed).astype(bf16)
    digits = jnp.concatenate([labels // 32, labels % 32]).astype(bf16)
    digits = jnp.where(mp_index == 0, digits, 0)
    extra = jnp.zeros((8, width), bf16).at[0, : 2 * query_count].set(digits)
    tables = group_tables(jnp.concatenate([table, extra]))
    all_count = data_ways * query_count
    query_cls = tables[:, :query_count].reshape(all_count, width)
    passage_cls = tables[:, query_count : 2 * query_count].reshape(all_count, width)
    digits = tables[:, 2 * query_count, : 2 * query_count].astype(jnp.int32)
    all_labels = (digits[:, :query_count] * 32 + digits[:, query_count:]).reshape(-1)

    logits = mm(query_cls, passage_cls, NT) * temper
    targets = all_labels[:, None] == jnp.arange(all_count, dtype=jnp.int32)[None, :]
    top = jnp.max(logits, axis=1, keepdims=True)
    raised = jnp.exp(logits - top)
    total = jnp.sum(raised, axis=1, keepdims=True)
    losses = top[:, 0] + jnp.log(total[:, 0]) - jnp.sum(jnp.where(targets, logits, 0.0), axis=1)
    query_losses = lax.dynamic_slice_in_dim(losses, data_index * query_count, query_count)
    grad_logits = (raised / total - targets.astype(f32)) * temper
    rows_of = lax.dynamic_slice_in_dim(grad_logits, data_index * query_count, query_count, 0)
    columns_of = lax.dynamic_slice_in_dim(grad_logits, data_index * query_count, query_count, 1)
    grad_cls = jnp.concatenate(
        [
            jnp.dot(rows_of, passage_cls.astype(f32), precision=highest),
            jnp.dot(columns_of.T, query_cls.astype(f32), precision=highest),
        ]
    )
    grad_mixed = grad_out.astype(f32) + jnp.dot(
        picker.astype(f32).T, grad_cls, precision=highest
    )

    grad_second = norm_pull(grad_mixed, unit_two, inverse_two, ln2_gain)
    stats = [
        jnp.sum(grad_mixed * unit_two, axis=0, keepdims=True),
        jnp.sum(grad_mixed, axis=0, keepdims=True),
        jnp.sum(grad_second, axis=0, keepdims=True),
    ]
    second_low = grad_second.astype(bf16)

    def to_core(left, right):
        return mm(left[:, left.shape[1] // 2 :], right, TN).astype(bf16)

    def chip_sum(left, right, arrived):
        own = mm(left[:, : left.shape[1] // 2], right, TN)
        return add(own, arrived).reshape(2, 2, ways, piece_rows, width)

    back_sent = to_core(active, second_low)
    back_arrived = swap(back_sent, CORE)
    pulled, back_sent = lax.optimization_barrier((second_low, back_sent))
    grad_before = (mm(pulled, back_all, NT) * slope.astype(f32)).astype(bf16)
    back_sum = chip_sum(active, second_low, back_arrived)
    back_half = swap(back_sum[1], NEAR_Y)
    in_sent = to_core(grad_before, hidden_low)
    in_arrived = swap(in_sent, CORE)
    pulled = after(grad_before, back_sum, in_sent)
    grad_hidden = grad_second + mm(pulled, in_all)
    grad_first = norm_pull(grad_hidden, unit_one, inverse_one, ln1_gain)
    stats += [
        jnp.sum(grad_hidden * unit_one, axis=0, keepdims=True),
        jnp.sum(grad_hidden, axis=0, keepdims=True),
        jnp.sum(grad_first, axis=0, keepdims=True),
    ]
    first_low = grad_first.astype(bf16)
    first_before, first_after = halo_rows(first_low, halo)
    in_sum = chip_sum(after(grad_before, first_low), hidden_low, in_arrived)
    in_half = swap(in_sum[:, 1], NEAR_X)
    out_keep, out_sent = local(
        functools.partial(out_grads_kernel, ways), place, (context, first_low),
        [((4 * ways, part + 8, width), bf16)] * 2, [((8 * ways, part + 8, width), f32)], 3, "out_grads",
    )
    out_sum = add(out_keep, swap(out_sent, CORE)).reshape(2, 2, ways, part + 8, width)
    out_half = swap(out_sum[1], NEAR_Y)

    d_b_in = jnp.sum(grad_before, axis=0, dtype=f32, keepdims=True)
    (vectors,) = local(
        vectors_kernel, place, (*stats, d_b_in), [((ways, 8, width), f32)],
        [((ways * PLANE, 8, 128), f32)], 2, "vectors",
    )

    first_before, first_after = after((first_before, first_after), in_sum, out_sent, vectors)
    first_window = jnp.concatenate([first_before, first_low, first_after])
    grad_context = mm(first_window, out_all, NT).astype(bf16)
    grad_context = after(grad_context, in_sum, back_sum, out_sum, vectors)
    grad_query, *sums = attend_backward(bounds, queries, keys, values, grad_context, halo, ())
    back_half, in_half, out_half = after((back_half, in_half, out_half), grad_query)
    back_sum = add(back_sum[0], back_half)
    in_sum = add(in_sum[:, 0], in_half)
    out_sum = add(out_sum[0], out_half)
    back_half = swap(back_sum[1], NEAR_X)
    in_half = swap(in_sum[1], NEAR_Y)
    out_half = swap(out_sum[1], NEAR_X)
    grad_context = after(grad_context, back_sum, in_sum, out_sum, grad_query)
    late_query, grad_keys, grad_values = attend_backward(
        bounds, queries, keys, values, grad_context, halo, sums
    )
    halves = [(back_sum[0], back_half), (in_sum[0], in_half), (out_sum[0], out_half)]
    halves = after(halves, late_query)
    early_sum = jnp.concatenate([add(*half) for half in halves], axis=1)
    early_parts = [early_sum[i] for i in range(ways)]
    early_odd = jnp.stack(early_parts[1::2])
    tokens_low, early_odd = lax.optimization_barrier((tokens, early_odd))
    early_odd = partner(early_odd, 1)

    late_rows = 3 * part + 8
    late_keep, late_sent = local(
        piece_grads_kernel, place, (grad_query, late_query, grad_keys, grad_values, tokens_low, vectors),
        [((4 * ways, late_rows, width), bf16)] * 2, [((8 * ways, late_rows, width), f32)], 8, "piece_grads", 36,
    )
    late_sum = add(late_keep, swap(late_sent, CORE)).reshape(2, 2, ways, late_rows, width)
    halves = first_sum_step(late_sum)
    early_odd = after(early_odd, late_sum)
    early_parts = [add(even, odd) for even, odd in zip(early_parts[::2], early_odd)]
    halves = second_sum_step(halves)
    late_parts = [half[i] for half in (add(*h) for h in halves) for i in range(ways // 2)]
    level, early_own = 2, early_parts[0].astype(f32)
    while level < ways:
        early_own = early_own + after(partner(early_parts[level // 2], level), late_parts).astype(f32)
        level *= 2
    late_total = sum_along(late_parts)
    early_held = second_step(first_step(over_groups(early_own).astype(bf16)[None], late_total))
    grad_queries = jnp.concatenate([grad_query, late_query])
    d_tokens = (
        grad_first
        + mm(grad_queries, qkv_all[:width])
        + mm(grad_keys, qkv_all[width : 2 * width])
        + mm(grad_values, qkv_all[2 * width :])
    )
    late_held = first_step(late_total.astype(bf16)[None])
    early_pieces = core_step(after(early_held, late_held))
    late_pieces = core_step(second_step(late_held, d_tokens))
    line = late_total[3 * part :]

    d_query, d_key, d_value = local(
        finish_heads_kernel, place, late_pieces, [((inner, width), f32)] * 3,
        [((PLANE, 3 * part, width), f32)], 4, "finish_heads",
    )
    d_back, d_in, d_out = local(
        finish_units_kernel, place, early_pieces,
        [((units, width), f32), ((width, units), f32), ((inner, width), f32)],
        [((PLANE, 2 * piece_rows + part + 8, width), f32), ((units, width), f32)], 6, "finish_units",
    )
    norms = [line[1 + i // ways, i % ways * inner : (i % ways + 1) * inner] for i in range(8)]
    return (
        mixed,
        query_losses,
        d_tokens,
        d_query.T,
        d_key.T,
        d_value.T,
        norms[6],
        norms[7],
        d_out,
        norms[5],
        norms[3],
        norms[4],
        d_in,
        line[0],
        d_back,
        norms[2],
        norms[0],
        norms[1],
    )


def solution(mesh):
    return jax.shard_map(
        shards,
        mesh=mesh,
        in_specs=(
            P(("dp", "mp"), None), P(("dp", "mp"), None), P("dp", None), P("dp"),
            P(None, "mp"), P(None, "mp"), P(None, "mp"), P("mp"), P("mp"), P("mp", None), P(),
            P(), P(), P(None, "mp"), P("mp"), P("mp", None), P(), P(), P(),
        ),
        out_specs=(
            P(("dp", "mp"), None), P("dp"), P(("dp", "mp"), None),
            P(None, "mp"), P(None, "mp"), P(None, "mp"), P("mp"), P("mp"), P("mp", None),
            P("mp"), P("mp"), P("mp"), P(None, "mp"), P("mp"), P("mp", None), P("mp"), P("mp"), P("mp"),
        ),
        check_vma=False,
    )
```

profile of v0, /device:TPU:1, one launch (start us, length us, event | category | flops | bytes accessed | tf_op | source)
XLA Modules:
  0.0 372.3 jit_solution(18023015296821944157)
XLA Ops:
  7.1 4.2 %collective-permute-start.2 = (bf16[80,768]{1,0:T(8,128)(2,1)S(1)}, bf16[80,768]{1,0:T(8,128)(2,1)S(1)}, u32[]{:S(2)}, u32[]{:S(2)}) collective-permute-start(bf16[80,768]{1,0:T(8,128)(2,1)S(1)} %fusion.44), channel_id=1, source_target_pairs={{0,3},{1,2},{2,1},{3,0},{4,7},{5,6},{6,5},{7,4},{8,11},{9,10},{10,... | collective-permute-start | bytes 368648 | tf_op jit(solution)/shard_map/ppermute | solution.py:594
  14.4 6.9 %collective-permute-done.1 = bf16[80,768]{1,0:T(8,128)(2,1)S(1)} collective-permute-done((bf16[80,768]{1,0:T(8,128)(2,1)S(1)}, bf16[80,768]{1,0:T(8,128)(2,1)S(1)}, u32[]{:S(2)}, u32[]{:S(2)}) %collective-permute-start.1) | collective-permute-done | bytes 122912 | tf_op jit(solution)/shard_map/ppermute | solution.py:594
  25.4 4.8 %collective-permute-start.5 = (bf16[256,768]{1,0:T(8,128)(2,1)S(1)}, bf16[256,768]{1,0:T(8,128)(2,1)S(1)}, u32[]{:S(2)}, u32[]{:S(2)}) collective-permute-start(bf16[256,768]{1,0:T(8,128)(2,1)S(1)} %get-tuple-element.261), channel_id=1, source_target_pairs={{0,1},{1,2},{2,3},{4,5},{5,6},{6,7},{8,9},{9,10},{10,11},{12,13},{... | collective-permute-start | bytes 1179656 | tf_op jit(solution)/shard_map/ppermute | solution.py:599
  30.3 11.6 %collective-permute-done.6 = bf16[1,224,768]{2,1,0:T(8,128)(2,1)S(1)} collective-permute-done((bf16[1,224,768]{2,1,0:T(8,128)(2,1)S(1)}, bf16[1,224,768]{2,1,0:T(8,128)(2,1)S(1)}, u32[]{:S(2)}, u32[]{:S(2)}) %collective-permute-start.6) | collective-permute-done | bytes 344096 | tf_op jit(solution)/shard_map/ppermute | solution.py:594
  51.9 7.7 %collective-permute-done.7 = bf16[2,224,768]{2,1,0:T(8,128)(2,1)} collective-permute-done((bf16[2,224,768]{2,1,0:T(8,128)(2,1)}, bf16[2,224,768]{2,1,0:T(8,128)(2,1)}, u32[]{:S(2)}, u32[]{:S(2)}) %collective-permute-start.7) | collective-permute-done | bytes 688160 | tf_op jit(solution)/shard_map/ppermute | solution.py:594
  70.2 6.7 %project.1 = (bf16[1280,768]{1,0:T(8,128)(2,1)S(1)}, bf16[1280,768]{1,0:T(8,128)(2,1)S(1)}, bf16[1280,768]{1,0:T(8,128)(2,1)S(1)}, bf16[2304,768]{1,0:T(8,128)(2,1)S(1)}) custom-call(s32[2]{0:T(128)S(1)} %pad_add_fusion.place_ref, bf16[256,768]{1,0:T(8,128)(2,1)S(1)} %copy-done.40, bf16[768,768]{1,0:T(8,128)(2,1)S(1)} %copy-done.5, ...), custom_call_target="tpu_custom_call" | custom-call | flops 200000000 | bytes 700000 | tf_op jit(solution)/shard_map/project/pallas_call | solution.py:285
  79.7 5.1 %attend_forward.2 = bf16[384,768]{1,0:T(8,128)(2,1)S(1)} custom-call(s32[3,20]{1,0:T(4,128)S(1)} %get-tuple-element.131.tiles_ref, s32[1,1280]{1,0:T(1,128)S(1)} %get-tuple-element.132.lo_ref, s32[1,1280]{1,0:T(1,128)S(1)} %get-tuple-element.133.hi_ref, bf16[1280,768]{1,0:T(8,128)(2,1)S(1)} %get-tuple-element.165.q_ref, ...), custom_call_target="tpu_custom_call" | custom-call | flops 140000000 | bytes 490000 | tf_op jit(solution)/shard_map/attend_forward/pallas_call | solution.py:189
  84.9 6.1 %collective-permute-done.14.refs_1_ = bf16[2,3,64,768]{3,2,1,0:T(8,128)(2,1)S(1)} collective-permute-done((bf16[2,3,64,768]{3,2,1,0:T(8,128)(2,1)S(1)}, bf16[2,3,64,768]{3,2,1,0:T(8,128)(2,1)S(1)}, u32[]{:S(2)}, u32[]{:S(2)}) %collective-permute-start.14) | collective-permute-done | bytes 589856 | tf_op jit(solution)/shard_map/ppermute | solution.py:628
  103.1 6.2 %attend_forward.3 = bf16[384,768]{1,0:T(8,128)(2,1)S(1)} custom-call(s32[3,20]{1,0:T(4,128)S(1)} %get-tuple-element.131.tiles_ref, s32[1,1280]{1,0:T(1,128)S(1)} %get-tuple-element.132.lo_ref, s32[1,1280]{1,0:T(1,128)S(1)} %get-tuple-element.133.hi_ref, bf16[1280,768]{1,0:T(8,128)(2,1)S(1)} %get-tuple-element.165.q_ref, bf16[1280,768]{1,0:T(8,128)(2,1)S(1)} %copy-done.1, ...), custom_call_target="tpu_custom_call" | custom-call | flops 140000000 | bytes 490000 | tf_op jit(solution)/shard_map/attend_forward/pallas_call | solution.py:189
  137.1 9.4 %fusion.4 = (bf16[768,3072]{1,0:T(8,128)(2,1)}, bf16[768,3072]{1,0:T(8,128)(2,1)S(1)}) fusion(f32[3072]{0:T(1024)S(1)} %bitcast.255, bf16[768,768]{1,0:T(8,128)(2,1)S(1)} %fusion.17, bf16[3072,768]{1,0:T(8,128)(2,1)S(1)} %bitcast.252), kind=kOutput, calls=%fused_computation.5 | convolution fusion | flops 3652190208 | bytes 15347712 | tf_op jit(solution)/shard_map/dot_general | solution.py:32
  149.6 4.1 %fusion.87 = (f32[768]{0:T(1024)S(1)}, f32[768,768]{1,0:T(8,128)S(1)}) fusion(f32[768]{0:T(1024)S(1)} %copy-done.70, bf16[768,3072]{1,0:T(8,128)(2,1)S(1)} %get-tuple-element.175, bf16[3072,768]{1,0:T(8,128)(2,1)S(1)} %join_back.1, f32[768]{0:T(1024)S(1)} %copy-done.67, f32[768]{0:T(1024)S(1)} %copy-done.66, f32[768]{0:T(1024)S(1)} %add_rsqrt_fusion.1, ...), kind=kOutput, calls=%fused_computation.227 | convolution fusion | flops 3628006656 | bytes 14174208 | tf_op jit(solution)/shard_map/dot_general | solution.py:32
  173.0 4.5 %collective-permute-done.27 = bf16[4,32,768]{2,1,0:T(8,128)(2,1)} collective-permute-done((bf16[4,32,768]{2,1,0:T(8,128)(2,1)S(1)}, bf16[4,32,768]{2,1,0:T(8,128)(2,1)}, u32[]{:S(2)}, u32[]{:S(2)}) %collective-permute-start.27) | collective-permute-done | bytes 196640 | tf_op jit(solution)/shard_map/ppermute | solution.py:614
  181.3 4.3 %multiply_reduce_fusion.1 = (f32[768]{0:T(1024)S(1)}, f32[768]{0:T(1024)S(1)}, f32[768]{0:T(1024)S(1)}, f32[768]{0:T(1024)S(1)}, f32[768,768]{1,0:T(8,128)S(1)}) fusion(f32[768,768]{1,0:T(8,128)} %copy-done.55, f32[768]{0:T(1024)S(1)} %add_rsqrt_fusion, f32[768]{0:T(1024)S(1)} %broadcast_multiply_fusion.4, f32[768]{0:T(1024)S(1)} %copy-done.65, ...), kind=kOutput, calls=%fused_computation.24 | convolution fusion | flops 176391168 | bytes 5993568 | tf_op jit(solution)/shard_map/dot_general | solution.py:833
  191.0 7.5 %convert_reduce_fusion = (f32[3072]{0:T(1024)S(1)}, bf16[768,3072]{1,0:T(8,128)(2,1)}) fusion(bf16[768,3072]{1,0:T(8,128)(2,1)} %get-tuple-element.177, bf16[768,768]{1,0:T(8,128)(2,1)S(1)} %convert_element_type.275, bf16[3072,768]{1,0:T(8,128)(2,1)S(1)} %bitcast.228), kind=kOutput, calls=%fused_computation.6 | convolution fusion | flops 3635672064 | bytes 15347712 | tf_op jit(solution)/shard_map/dot_general | solution.py:32
  206.5 4.5 %multiply_reduce_fusion = (f32[768]{0:T(1024)S(1)}, f32[768]{0:T(1024)S(1)}, f32[768]{0:T(1024)S(1)}, f32[768]{0:T(1024)S(1)}, f32[768,768]{1,0:T(8,128)S(1)}) fusion(f32[768,768]{1,0:T(8,128)S(1)} %copy-done.54, f32[768]{0:T(1024)S(1)} %add_rsqrt_fusion.1, f32[768]{0:T(1024)S(1)} %broadcast_multiply_fusion.5, f32[768]{0:T(1024)S(1)} %copy-done.66, ...), kind=kOutput, calls=%fused_computation.23 | convolution fusion | flops 3629773824 | bytes 16536576 | tf_op jit(solution)/shard_map/dot_general | solution.py:32
  231.7 14.4 %attend_backward.2 = (bf16[384,768]{1,0:T(8,128)(2,1)S(1)}, f32[1280,768]{1,0:T(8,128)}, f32[1280,768]{1,0:T(8,128)}) custom-call(s32[3,20]{1,0:T(4,128)S(1)} %get-tuple-element.131.tiles_ref, s32[1,1280]{1,0:T(1,128)S(1)} %get-tuple-element.132.lo_ref, s32[1,1280]{1,0:T(1,128)S(1)} %get-tuple-element.133.hi_ref, ...), custom_call_target="tpu_custom_call" | custom-call | flops 320000000 | bytes 1120000 | tf_op jit(solution)/shard_map/attend_backward/pallas_call | solution.py:189
  246.1 5.5 %collective-permute-done.33 = bf16[2,4,96,768]{3,2,1,0:T(8,128)(2,1)} collective-permute-done((bf16[2,4,96,768]{3,2,1,0:T(8,128)(2,1)}, bf16[2,4,96,768]{3,2,1,0:T(8,128)(2,1)}, u32[]{:S(2)}, u32[]{:S(2)}) %collective-permute-start.33) | collective-permute-done | bytes 1179680 | tf_op jit(solution)/shard_map/ppermute | solution.py:628
  253.4 8.3 %collective-permute-done.35 = bf16[2,4,32,768]{3,2,1,0:T(8,128)(2,1)S(1)} collective-permute-done((bf16[2,4,32,768]{3,2,1,0:T(8,128)(2,1)S(1)}, bf16[2,4,32,768]{3,2,1,0:T(8,128)(2,1)S(1)}, u32[]{:S(2)}, u32[]{:S(2)}) %collective-permute-start.35) | collective-permute-done | bytes 393248 | tf_op jit(solution)/shard_map/ppermute | solution.py:628
  268.2 22.0 %attend_backward.3 = (bf16[384,768]{1,0:T(8,128)(2,1)S(1)}, bf16[768,768]{1,0:T(8,128)(2,1)S(1)}, bf16[768,768]{1,0:T(8,128)(2,1)S(1)}) custom-call(s32[3,20]{1,0:T(4,128)S(1)} %get-tuple-element.131.tiles_ref, s32[1,1280]{1,0:T(1,128)S(1)} %get-tuple-element.132.lo_ref, s32[1,1280]{1,0:T(1,128)S(1)} %get-tuple-element.133.hi_ref, ...), custom_call_target="tpu_custom_call" | custom-call | flops 320000000 | bytes 1120000 | tf_op jit(solution)/shard_map/attend_backward/pallas_call | solution.py:189
  290.9 4.7 %piece_grads.1 = (bf16[16,80,768]{2,1,0:T(8,128)(2,1)S(1)}, bf16[16,80,768]{2,1,0:T(8,128)(2,1)S(1)}) custom-call(s32[2]{0:T(128)S(1)} %pad_add_fusion.place_ref, bf16[384,768]{1,0:T(8,128)(2,1)S(1)} %get-tuple-element.184.dq_first_ref, bf16[384,768]{1,0:T(8,128)(2,1)S(1)} %get-tuple-element.192.dq_second_ref, ...), custom_call_target="tpu_custom_call" | custom-call | flops 160000000 | bytes 560000 | tf_op jit(solution)/shard_map/piece_grads/pallas_call | solution.py:285
  302.7 9.6 %collective-permute-done.52 = bf16[2,224,768]{2,1,0:T(8,128)(2,1)S(1)} collective-permute-done((bf16[2,224,768]{2,1,0:T(8,128)(2,1)S(1)}, bf16[2,224,768]{2,1,0:T(8,128)(2,1)S(1)}, u32[]{:S(2)}, u32[]{:S(2)}) %collective-permute-start.52) | collective-permute-done | bytes 688160 | tf_op jit(solution)/shard_map/ppermute | solution.py:594
  316.1 4.9 %collective-permute-done.44 = bf16[2,80,768]{2,1,0:T(8,128)(2,1)S(1)} collective-permute-done((bf16[2,80,768]{2,1,0:T(8,128)(2,1)S(1)}, bf16[2,80,768]{2,1,0:T(8,128)(2,1)S(1)}, u32[]{:S(2)}, u32[]{:S(2)}) %collective-permute-start.44) | collective-permute-done | bytes 245792 | tf_op jit(solution)/shard_map/ppermute | solution.py:628
  324.1 15.3 %collective-permute-done.53 = bf16[224,768]{1,0:T(8,128)(2,1)S(1)} collective-permute-done((bf16[224,768]{1,0:T(8,128)(2,1)S(1)}, bf16[224,768]{1,0:T(8,128)(2,1)S(1)}, u32[]{:S(2)}, u32[]{:S(2)}) %collective-permute-start.53) | collective-permute-done | bytes 344096 | tf_op jit(solution)/shard_map/ppermute | solution.py:594
  347.8 4.7 %collective-permute-done.57 = bf16[2,1,112,768]{3,2,0,1:T(8,128)(2,1)S(1)} collective-permute-done((bf16[2,1,112,768]{3,2,0,1:T(8,128)(2,1)S(1)}, bf16[2,1,112,768]{3,2,0,1:T(8,128)(2,1)S(1)}, u32[]{:S(2)}, u32[]{:S(2)}) %collective-permute-start.57) | collective-permute-done | bytes 344096 | tf_op jit(solution)/shard_map/ppermute | solution.py:628
  (426 shorter events, 186.5 us)
Async XLA Ops:
  24.0 17.9 %collective-permute-start.6 = (bf16[1,224,768]{2,1,0:T(8,128)(2,1)S(1)}, bf16[1,224,768]{2,1,0:T(8,128)(2,1)S(1)}, u32[]{:S(2)}, u32[]{:S(2)}) collective-permute-start(bf16[1,224,768]{2,1,0:T(8,128)(2,1)S(1)} %bitcast.264), channel_id=1, source_target_pairs={{0,2},{1,3},{2,0},{3,1},{4,6},{5,7},{6,4},{7,5},{8,10},{9,11},{10,... | collective-permute-start | bytes 1032200 | tf_op jit(solution)/shard_map/ppermute | solution.py:594
  24.1 18.8 %collective-permute-start.8 = (bf16[256,768]{1,0:T(8,128)(2,1)S(1)}, bf16[256,768]{1,0:T(8,128)(2,1)S(1)}, u32[]{:S(2)}, u32[]{:S(2)}) collective-permute-start(bf16[256,768]{1,0:T(8,128)(2,1)S(1)} %get-tuple-element.260), channel_id=1, source_target_pairs={{1,0},{2,1},{3,2},{5,4},{6,5},{7,6},{9,8},{10,9},{11,10},{13,12},{... | collective-permute-start | bytes 1179656 | tf_op jit(solution)/shard_map/ppermute | solution.py:600
  25.4 18.3 %collective-permute-start.5 = (bf16[256,768]{1,0:T(8,128)(2,1)S(1)}, bf16[256,768]{1,0:T(8,128)(2,1)S(1)}, u32[]{:S(2)}, u32[]{:S(2)}) collective-permute-start(bf16[256,768]{1,0:T(8,128)(2,1)S(1)} %get-tuple-element.261), channel_id=1, source_target_pairs={{0,1},{1,2},{2,3},{4,5},{5,6},{6,7},{8,9},{9,10},{10,11},{12,13},{... | collective-permute-start | bytes 1179656 | tf_op jit(solution)/shard_map/ppermute | solution.py:599
  42.9 16.7 %collective-permute-start.7 = (bf16[2,224,768]{2,1,0:T(8,128)(2,1)}, bf16[2,224,768]{2,1,0:T(8,128)(2,1)}, u32[]{:S(2)}, u32[]{:S(2)}) collective-permute-start(bf16[2,224,768]{2,1,0:T(8,128)(2,1)} %pad_maximum_fusion.7), channel_id=1, source_target_pairs={{0,1},{1,0},{2,3},{3,2},{4,5},{5,4},{6,7},{7,6},{8,9},{9,8},{10,11... | collective-permute-start | bytes 2064392 | tf_op jit(solution)/shard_map/ppermute | solution.py:594
  77.0 14.0 %collective-permute-start.14 = (bf16[2,3,64,768]{3,2,1,0:T(8,128)(2,1)S(1)}, bf16[2,3,64,768]{3,2,1,0:T(8,128)(2,1)S(1)}, u32[]{:S(2)}, u32[]{:S(2)}) collective-permute-start(bf16[2,3,64,768]{3,2,1,0:T(8,128)(2,1)S(1)} %get-tuple-element.271.refs_0_), channel_id=1, source_target_pairs={{0,16},{4,20},{8,24},{12,28},{16,0},{20,4},{24,8},{28,12},{1,17},{... | collective-permute-start | bytes 1769480 | tf_op jit(solution)/shard_map/ppermute | solution.py:628
  93.8 22.2 %collective-permute-start.16 = (bf16[4,2,3,64,768]{4,3,2,1,0:T(8,128)(2,1)}, bf16[4,2,3,64,768]{4,3,2,1,0:T(8,128)(2,1)}, u32[]{:S(2)}, u32[]{:S(2)}) collective-permute-start(bf16[4,2,3,64,768]{4,3,2,1,0:T(8,128)(2,1)} %pad_maximum_fusion), channel_id=1, source_target_pairs={{0,4},{4,0},{8,12},{12,8},{16,20},{20,16},{24,28},{28,24},{1,5},{5... | collective-permute-start | bytes 7077896 | tf_op jit(solution)/shard_map/ppermute | solution.py:628
  112.5 20.1 %collective-permute-start.19 = (bf16[2,3,48,768]{3,2,1,0:T(8,128)(2,1)}, bf16[2,3,48,768]{3,2,1,0:T(8,128)(2,1)}, u32[]{:S(2)}, u32[]{:S(2)}) collective-permute-start(bf16[2,3,48,768]{3,2,1,0:T(8,128)(2,1)} %get-tuple-element.275.refs_0_), channel_id=1, source_target_pairs={{0,16},{4,20},{8,24},{12,28},{16,0},{20,4},{24,8},{28,12},{1,17},{... | collective-permute-start | bytes 1327112 | tf_op jit(solution)/shard_map/ppermute | solution.py:628
  115.8 16.7 %collective-permute-start.20 = (bf16[2,3,48,768]{3,2,1,0:T(8,128)(2,1)}, bf16[2,3,48,768]{3,2,1,0:T(8,128)(2,1)}, u32[]{:S(2)}, u32[]{:S(2)}) collective-permute-start(bf16[2,3,48,768]{3,2,1,0:T(8,128)(2,1)} %get-tuple-element.277.refs_2_), channel_id=1, source_target_pairs={{0,8},{4,12},{8,0},{12,4},{16,24},{20,28},{24,16},{28,20},{1,9},{5... | collective-permute-start | bytes 1327112 | tf_op jit(solution)/shard_map/ppermute | solution.py:628
  202.3 18.1 %collective-permute-start.31 = (bf16[1536,768]{1,0:T(8,128)(2,1)S(1)}, bf16[1536,768]{1,0:T(8,128)(2,1)S(1)}, u32[]{:S(2)}, u32[]{:S(2)}) collective-permute-start(bf16[1536,768]{1,0:T(8,128)(2,1)S(1)} %convolution_convert_fusion), channel_id=1, source_target_pairs={{0,4},{4,0},{8,12},{12,8},{16,20},{20,16},{24,28},{28,24},{1,5},{5... | collective-permute-start | bytes 7077896 | tf_op jit(solution)/shard_map/ppermute | solution.py:628
  212.2 15.8 %collective-permute-start.30 = (bf16[256,768]{1,0:T(8,128)(2,1)S(1)}, bf16[256,768]{1,0:T(8,128)(2,1)S(1)}, u32[]{:S(2)}, u32[]{:S(2)}) collective-permute-start(bf16[256,768]{1,0:T(8,128)(2,1)S(1)} %get-tuple-element.258), channel_id=1, source_target_pairs={{1,0},{2,1},{3,2},{5,4},{6,5},{7,6},{9,8},{10,9},{11,10},{13,12},{... | collective-permute-start | bytes 1179656 | tf_op jit(solution)/shard_map/ppermute | solution.py:600
  213.6 14.4 %collective-permute-start.29 = (bf16[256,768]{1,0:T(8,128)(2,1)S(1)}, bf16[256,768]{1,0:T(8,128)(2,1)S(1)}, u32[]{:S(2)}, u32[]{:S(2)}) collective-permute-start(bf16[256,768]{1,0:T(8,128)(2,1)S(1)} %get-tuple-element.259), channel_id=1, source_target_pairs={{0,1},{1,2},{2,3},{4,5},{5,6},{6,7},{8,9},{9,10},{10,11},{12,13},{... | collective-permute-start | bytes 1179656 | tf_op jit(solution)/shard_map/ppermute | solution.py:599
  223.7 27.9 %collective-permute-start.33 = (bf16[2,4,96,768]{3,2,1,0:T(8,128)(2,1)}, bf16[2,4,96,768]{3,2,1,0:T(8,128)(2,1)}, u32[]{:S(2)}, u32[]{:S(2)}) collective-permute-start(bf16[2,4,96,768]{3,2,1,0:T(8,128)(2,1)} %slice_bitcast_fusion.1), channel_id=1, source_target_pairs={{0,8},{4,12},{8,0},{12,4},{16,24},{20,28},{24,16},{28,20},{1,9},{5... | collective-permute-start | bytes 3538952 | tf_op jit(solution)/shard_map/ppermute | solution.py:628
  225.9 27.6 %collective-permute-start.32 = (bf16[2,4,96,768]{3,2,1,0:T(8,128)(2,1)}, bf16[2,4,96,768]{3,2,1,0:T(8,128)(2,1)}, u32[]{:S(2)}, u32[]{:S(2)}) collective-permute-start(bf16[2,4,96,768]{3,2,1,0:T(8,128)(2,1)} %bitcast.52), channel_id=1, source_target_pairs={{0,16},{4,20},{8,24},{12,28},{16,0},{20,4},{24,8},{28,12},{1,17},{... | collective-permute-start | bytes 3538952 | tf_op jit(solution)/shard_map/ppermute | solution.py:628
  228.3 33.5 %collective-permute-start.35 = (bf16[2,4,32,768]{3,2,1,0:T(8,128)(2,1)S(1)}, bf16[2,4,32,768]{3,2,1,0:T(8,128)(2,1)S(1)}, u32[]{:S(2)}, u32[]{:S(2)}) collective-permute-start(bf16[2,4,32,768]{3,2,1,0:T(8,128)(2,1)S(1)} %bitcast.266), channel_id=1, source_target_pairs={{0,16},{4,20},{8,24},{12,28},{16,0},{20,4},{24,8},{28,12},{1,17},{... | collective-permute-start | bytes 1179656 | tf_op jit(solution)/shard_map/ppermute | solution.py:628
  265.2 25.1 %collective-permute-start.36 = (bf16[4,96,768]{2,1,0:T(8,128)(2,1)S(1)}, bf16[4,96,768]{2,1,0:T(8,128)(2,1)S(1)}, u32[]{:S(2)}, u32[]{:S(2)}) collective-permute-start(bf16[4,96,768]{2,1,0:T(8,128)(2,1)S(1)} %get-tuple-element.256), channel_id=1, source_target_pairs={{0,8},{4,12},{8,0},{12,4},{16,24},{20,28},{24,16},{28,20},{1,9},{5... | collective-permute-start | bytes 1769480 | tf_op jit(solution)/shard_map/ppermute | solution.py:628
  265.8 24.5 %collective-permute-start.37 = (bf16[4,96,768]{2,1,0:T(8,128)(2,1)S(1)}, bf16[4,96,768]{2,1,0:T(8,128)(2,1)S(1)}, u32[]{:S(2)}, u32[]{:S(2)}) collective-permute-start(bf16[4,96,768]{2,1,0:T(8,128)(2,1)S(1)} %get-tuple-element.254), channel_id=1, source_target_pairs={{0,16},{4,20},{8,24},{12,28},{16,0},{20,4},{24,8},{28,12},{1,17},{... | collective-permute-start | bytes 1769480 | tf_op jit(solution)/shard_map/ppermute | solution.py:628
  266.9 23.4 %collective-permute-start.38 = (bf16[4,32,768]{2,1,0:T(8,128)(2,1)S(1)}, bf16[4,32,768]{2,1,0:T(8,128)(2,1)S(1)}, u32[]{:S(2)}, u32[]{:S(2)}) collective-permute-start(bf16[4,32,768]{2,1,0:T(8,128)(2,1)S(1)} %get-tuple-element.282), channel_id=1, source_target_pairs={{0,8},{4,12},{8,0},{12,4},{16,24},{20,28},{24,16},{28,20},{1,9},{5... | collective-permute-start | bytes 589832 | tf_op jit(solution)/shard_map/ppermute | solution.py:628
  295.7 16.6 %collective-permute-start.52 = (bf16[2,224,768]{2,1,0:T(8,128)(2,1)S(1)}, bf16[2,224,768]{2,1,0:T(8,128)(2,1)S(1)}, u32[]{:S(2)}, u32[]{:S(2)}) collective-permute-start(bf16[2,224,768]{2,1,0:T(8,128)(2,1)S(1)} %pad_maximum_fusion.8), channel_id=1, source_target_pairs={{0,1},{1,0},{2,3},{3,2},{4,5},{5,4},{6,7},{7,6},{8,9},{9,8},{10,11... | collective-permute-start | bytes 2064392 | tf_op jit(solution)/shard_map/ppermute | solution.py:594
  300.2 13.8 %collective-permute-start.40 = (bf16[2,2,80,768]{3,2,1,0:T(8,128)(2,1)S(1)}, bf16[2,2,80,768]{3,2,1,0:T(8,128)(2,1)S(1)}, u32[]{:S(2)}, u32[]{:S(2)}) collective-permute-start(bf16[2,2,80,768]{3,2,1,0:T(8,128)(2,1)S(1)} %slice_bitcast_fusion.8), channel_id=1, source_target_pairs={{0,16},{4,20},{8,24},{12,28},{16,0},{20,4},{24,8},{28,12},{1,17},{... | collective-permute-start | bytes 1474568 | tf_op jit(solution)/shard_map/ppermute | solution.py:628
  315.9 23.5 %collective-permute-start.53 = (bf16[224,768]{1,0:T(8,128)(2,1)S(1)}, bf16[224,768]{1,0:T(8,128)(2,1)S(1)}, u32[]{:S(2)}, u32[]{:S(2)}) collective-permute-start(bf16[224,768]{1,0:T(8,128)(2,1)S(1)} %fusion.41), channel_id=1, source_target_pairs={{0,2},{1,3},{2,0},{3,1},{4,6},{5,7},{6,4},{7,5},{8,10},{9,11},{10,... | collective-permute-start | bytes 1032200 | tf_op jit(solution)/shard_map/ppermute | solution.py:594
  321.1 20.9 %collective-permute-start.45 = (bf16[80,768]{1,0:T(8,128)(2,1)S(1)}, bf16[80,768]{1,0:T(8,128)(2,1)S(1)}, u32[]{:S(2)}, u32[]{:S(2)}) collective-permute-start(bf16[80,768]{1,0:T(8,128)(2,1)S(1)} %get-tuple-element.302), channel_id=1, source_target_pairs={{0,2},{1,3},{2,0},{3,1},{4,6},{5,7},{6,4},{7,5},{8,10},{9,11},{10,... | collective-permute-start | bytes 368648 | tf_op jit(solution)/shard_map/ppermute | solution.py:594
  321.2 20.8 %collective-permute-start.46 = (bf16[80,768]{1,0:T(8,128)(2,1)S(1)}, bf16[80,768]{1,0:T(8,128)(2,1)S(1)}, u32[]{:S(2)}, u32[]{:S(2)}) collective-permute-start(bf16[80,768]{1,0:T(8,128)(2,1)S(1)} %get-tuple-element.303), channel_id=1, source_target_pairs={{0,3},{1,2},{2,1},{3,0},{4,7},{5,6},{6,5},{7,4},{8,11},{9,10},{10,... | collective-permute-start | bytes 368648 | tf_op jit(solution)/shard_map/ppermute | solution.py:594
  324.0 18.0 %collective-permute-start.42 = (bf16[80,768]{1,0:T(8,128)(2,1)S(1)}, bf16[80,768]{1,0:T(8,128)(2,1)S(1)}, u32[]{:S(2)}, u32[]{:S(2)}) collective-permute-start(bf16[80,768]{1,0:T(8,128)(2,1)S(1)} %slice_bitcast_fusion.20), channel_id=1, source_target_pairs={{0,1},{1,0},{2,3},{3,2},{4,5},{5,4},{6,7},{7,6},{8,9},{9,8},{10,11... | collective-permute-start | bytes 368648 | tf_op jit(solution)/shard_map/ppermute | solution.py:594
  352.8 15.3 %collective-permute-start.58 = (bf16[4,2,1,112,768]{4,3,2,1,0:T(8,128)(2,1)S(1)}, bf16[4,2,1,112,768]{4,3,2,1,0:T(8,128)(2,1)S(1)}, u32[]{:S(2)}, u32[]{:S(2)}) collective-permute-start(bf16[4,2,1,112,768]{4,3,2,1,0:T(8,128)(2,1)S(1)} %pad_maximum_fusion.4), channel_id=1, source_target_pairs={{0,4},{4,0},{8,12},{12,8},{16,20},{20,16},{24,28},{28,24},{1,5},{5... | collective-permute-start | bytes 4128776 | tf_op jit(solution)/shard_map/ppermute | solution.py:628
  (118 other events, 747.9 us)
where the time goes:
time: 378 us; the launch traced here: 372 us
  waiting for transfers between devices  115 us (30%)
  Pallas kernels  77.8 us (21%)
  starting transfers between devices  62.4 us (17%)
  matrix products  53.3 us (14%)
  local copies, waits for them, and re-layouts  37.8 us (10%)
  other arithmetic  23.6 us (6%)
    ppermute x13, waiting for transfers between devices, partner(): return lax.ppermute(values, 'mp', [(i, i ^ step) for i in range(ways)])  57.4 us
    ppermute x39, waiting for transfers between devices, swap(): return lax.ppermute(values, 'dp', [(i, i ^ bit) for i in range(ways)])  48.9 us
    dot_general x15, matrix products, mm(): return lax.dot_general(a, b, dims, preferred_element_type=f32)  48.5 us
    pallas_call x4, Pallas kernels, attention(): pl.pallas_call(kernel, out_shape=tuple((jax.ShapeDtypeStruct(shape, dtype...  47.8 us
    ppermute x39, starting transfers between devices, swap(): return lax.ppermute(values, 'dp', [(i, i ^ bit) for i in range(ways)])  35.2 us
    pallas_call x11, Pallas kernels, local(): pl.pallas_call(kernel, out_shape=tuple((jax.ShapeDtypeStruct(shape, dtype...  27.8 us
    unnamed x166, local copies, waits for them, and re-layouts  22.9 us
    ppermute x13, starting transfers between devices, partner(): return lax.ppermute(values, 'mp', [(i, i ^ step) for i in range(ways)])  12.7 us
  transfers between devices with their start and end apart: 59, of which 27 were waited for; matrix products, arithmetic and copies ran while one was open for 17% of the time, Pallas kernels for 18%

commit v1 on v0

--- a/solution.py
+++ b/solution.py
@@ -15,6 +15,7 @@
 TILE = 128
 QUERIES = 64
 QUAD = 4 * HEAD
+FIRST = 14 * QUERIES
 ALIGN = 32
 BLOCKS = (1, 2, 3, 4, 5, 7, 10)
 
@@ -203,7 +204,7 @@
     rows = (count - 2 * halo) // parts
     (context,) = attention(
         functools.partial(forward_kernel, halo, part * rows), (*bounds, queries, keys, values),
-        [((rows, width), bf16)], [((count, QUAD), f32)], 7, "attend_forward", 30,
+        [((rows, width), bf16)], [((count, QUAD), f32)], 7, "attend_forward", 14,
     )
     return context
 
@@ -254,8 +255,8 @@
         by_span(blocks, count, act)
         return carry
 
-    tiles = count // QUERIES // 2
-    lax.fori_loop(start // QUERIES, start // QUERIES + tiles, tile_step, 0)
+    end = count if carried else FIRST
+    lax.fori_loop(start // QUERIES, end // QUERIES, tile_step, 0)
     if carried:
         dk_ref[...] = dk_sum[pl.ds(halo, own), :].astype(bf16)
         dv_ref[...] = dv_sum[pl.ds(halo, own), :].astype(bf16)
@@ -265,14 +266,15 @@
     count, width = keys.shape
     own = count - 2 * halo
     window = ((count, width), f32)
-    outs = [((own // 2, width), bf16)]
+    rows = halo + own - FIRST if sums else FIRST - halo
+    outs = [((rows, width), bf16)]
     if sums:
         outs, scratch = outs + [((own, width), bf16)] * 2, [((count, QUAD), f32), window, window]
     else:
         outs, scratch = outs + [window, window], [((count, QUAD), f32)]
     return attention(
-        functools.partial(backward_kernel, halo, count // 2 if sums else 0, bool(sums)),
-        (*bounds, queries, keys, values, grads, *sums), outs, scratch, 16, "attend_backward", 48,
+        functools.partial(backward_kernel, halo, FIRST if sums else 0, bool(sums)),
+        (*bounds, queries, keys, values, grads, *sums), outs, scratch, 16, "attend_backward", 28,
     )
 
 
@@ -528,7 +530,7 @@
     ones = jnp.ones((8, tokens_ref.shape[0]), bf16)
     lines = jnp.zeros((8, width), f32)
     sums_of = (
-        mm(ones[:, :half], dq_first_ref[...]) + mm(ones[:, :half], dq_second_ref[...]),
+        mm(ones[:, :half], dq_first_ref[...]) + mm(ones[:, half:], dq_second_ref[...]),
         mm(ones, dv_ref[...]),
     )
     for sums, first in zip(sums_of, (width - 2 * inner, width - inner)):
@@ -779,17 +781,18 @@
         [((PLANE, part, width), f32)], 5, "join_in_out",
     )
     attended = mm(context, out_all)
-    back_held = second_step(first_step(back_start, context), attended)
+    first_sum = tokens.astype(f32) + attended + b_out
+    center_one, inverse_one = norm_parts(first_sum)
+    unit_one = center_one * inverse_one
+    hidden = unit_one * ln1_gain + ln1_shift
+    hidden_low = hidden.astype(bf16)
+    back_held = second_step(first_step(back_start, context), hidden_low)
     back_parts = core_step(back_held)
     (back_all,) = local(
         join_units_kernel, place, (back_own, *back_parts),
         [((ways * units, width), bf16)], [], 4, "join_back",
     )
-    first_sum = tokens.astype(f32) + attended + b_out
-    center_one, inverse_one = norm_parts(first_sum)
-    unit_one = center_one * inverse_one
-    hidden = unit_one * ln1_gain + ln1_shift
-    hidden_low = after(hidden.astype(bf16), back_held)
+    hidden_low = after(hidden_low, back_held)
 
     active, slope = gelu_both(mm(hidden_low, in_all, NT) + bias_in)
     active, slope = lax.optimization_barrier((active.astype(bf16), slope.astype(bf16)))
@@ -898,22 +901,22 @@
     late_query, grad_keys, grad_values = attend_backward(
         bounds, queries, keys, values, grad_context, halo, sums
     )
-    halves = [(back_sum[0], back_half), (in_sum[0], in_half), (out_sum[0], out_half)]
-    halves = after(halves, late_query)
-    early_sum = jnp.concatenate([add(*half) for half in halves], axis=1)
+    early_halves = [(back_sum[0], back_half), (in_sum[0], in_half), (out_sum[0], out_half)]
+    early_halves = after(early_halves, late_query)
+    early_sum = jnp.concatenate([add(*half) for half in early_halves], axis=1)
     early_parts = [early_sum[i] for i in range(ways)]
-    early_odd = jnp.stack(early_parts[1::2])
-    tokens_low, early_odd = lax.optimization_barrier((tokens, early_odd))
-    early_odd = partner(early_odd, 1)
+    tokens_low = after(tokens, early_parts)
 
     late_rows = 3 * part + 8
     late_keep, late_sent = local(
         piece_grads_kernel, place, (grad_query, late_query, grad_keys, grad_values, tokens_low, vectors),
         [((4 * ways, late_rows, width), bf16)] * 2, [((8 * ways, late_rows, width), f32)], 8, "piece_grads", 36,
     )
-    late_sum = add(late_keep, swap(late_sent, CORE)).reshape(2, 2, ways, late_rows, width)
+    late_arrived = swap(late_sent, CORE)
+    early_odd = partner(jnp.stack(early_parts[1::2]), 1)
+    late_sum = add(late_keep, late_arrived).reshape(2, 2, ways, late_rows, width)
     halves = first_sum_step(late_sum)
-    early_odd = after(early_odd, late_sum)
+    early_odd = after(early_odd, halves)
     early_parts = [add(even, odd) for even, odd in zip(early_parts[::2], early_odd)]
     halves = second_sum_step(halves)
     late_parts = [half[i] for half in (add(*h) for h in halves) for i in range(ways // 2)]

time: 378 us -> 369 us (0.976)
  waiting for transfers between devices: 115 us -> 134 us
  Pallas kernels: 77.8 us -> 63.6 us
  local copies, waits for them, and re-layouts: 37.8 us -> 25.1 us
  other arithmetic: 23.6 us -> 17.8 us
  starting transfers between devices: 62.4 us -> 66.4 us
    pallas_call x4, Pallas kernels: 47.8 us -> 33.2 us  [attention(): pl.pallas_call(kernel, out_shape=tuple((jax.ShapeDtypeStruct(shape, dtype...]
    ppermute x39, waiting for transfers between devices: 48.9 us -> 61.6 us  [swap(): return lax.ppermute(values, 'dp', [(i, i ^ bit) for i in range(ways)])]
    unnamed x166 -> x168, local copies, waits for them, and re-layouts: 22.9 us -> 16 us
    ppermute x39, starting transfers between devices: 35.2 us -> 40.8 us  [swap(): return lax.ppermute(values, 'dp', [(i, i ^ bit) for i in range(ways)])]
    ppermute x13, waiting for transfers between devices: 57.4 us -> 61.5 us  [partner(): return lax.ppermute(values, 'mp', [(i, i ^ step) for i in range(ways)])]
    another operation x11, other arithmetic: 7.92 us -> 3.87 us  [core_step(): return [*held, swap(jnp.stack(held), CORE)]]
  transfers between devices with their start and end apart: 59 -> 59, of which waited for: 27 -> 29; matrix products, arithmetic and copies ran while one was open for 17% -> 15% of each run, Pallas kernels for 18% -> 12%
where the time goes in v1:
time: 369 us; the launch traced here: 364 us
  waiting for transfers between devices  134 us (36%)
  starting transfers between devices  66.4 us (18%)
  Pallas kernels  63.6 us (17%)
  matrix products  54 us (15%)
  local copies, waits for them, and re-layouts  25.1 us (7%)
  other arithmetic  17.8 us (5%)
    ppermute x39, waiting for transfers between devices, swap(): return lax.ppermute(values, 'dp', [(i, i ^ bit) for i in range(ways)])  61.6 us
    ppermute x13, waiting for transfers between devices, partner(): return lax.ppermute(values, 'mp', [(i, i ^ step) for i in range(ways)])  61.5 us
    dot_general x15, matrix products, mm(): return lax.dot_general(a, b, dims, preferred_element_type=f32)  49.3 us
    ppermute x39, starting transfers between devices, swap(): return lax.ppermute(values, 'dp', [(i, i ^ bit) for i in range(ways)])  40.8 us
    pallas_call x4, Pallas kernels, attention(): pl.pallas_call(kernel, out_shape=tuple((jax.ShapeDtypeStruct(shape, dtype...  33.2 us
    pallas_call x11, Pallas kernels, local(): pl.pallas_call(kernel, out_shape=tuple((jax.ShapeDtypeStruct(shape, dtype...  28.1 us
    unnamed x168, local copies, waits for them, and re-layouts  16 us
    ppermute x13, starting transfers between devices, partner(): return lax.ppermute(values, 'mp', [(i, i ^ step) for i in range(ways)])  13.3 us
  transfers between devices with their start and end apart: 59, of which 29 were waited for; matrix products, arithmetic and copies ran while one was open for 15% of the time, Pallas kernels for 12%

profile of v1, /device:TPU:1, one launch (start us, length us, event | category | flops | bytes accessed | tf_op | source)
XLA Modules:
  0.0 363.8 jit_solution(9202200469145421970)
XLA Ops:
  14.4 6.9 %collective-permute-done.1 = bf16[80,768]{1,0:T(8,128)(2,1)S(1)} collective-permute-done((bf16[80,768]{1,0:T(8,128)(2,1)S(1)}, bf16[80,768]{1,0:T(8,128)(2,1)S(1)}, u32[]{:S(2)}, u32[]{:S(2)}) %collective-permute-start.1) | collective-permute-done | bytes 122912 | tf_op jit(solution)/shard_map/ppermute | solution.py:596
  25.4 4.8 %collective-permute-start.5 = (bf16[256,768]{1,0:T(8,128)(2,1)S(1)}, bf16[256,768]{1,0:T(8,128)(2,1)S(1)}, u32[]{:S(2)}, u32[]{:S(2)}) collective-permute-start(bf16[256,768]{1,0:T(8,128)(2,1)S(1)} %get-tuple-element.257), channel_id=1, source_target_pairs={{0,1},{1,2},{2,3},{4,5},{5,6},{6,7},{8,9},{9,10},{10,11},{12,13},{... | collective-permute-start | bytes 1179656 | tf_op jit(solution)/shard_map/ppermute | solution.py:601
  30.3 11.6 %collective-permute-done.6 = bf16[1,224,768]{2,1,0:T(8,128)(2,1)S(1)} collective-permute-done((bf16[1,224,768]{2,1,0:T(8,128)(2,1)S(1)}, bf16[1,224,768]{2,1,0:T(8,128)(2,1)S(1)}, u32[]{:S(2)}, u32[]{:S(2)}) %collective-permute-start.6) | collective-permute-done | bytes 344096 | tf_op jit(solution)/shard_map/ppermute | solution.py:596
  51.9 7.7 %collective-permute-done.7 = bf16[2,224,768]{2,1,0:T(8,128)(2,1)} collective-permute-done((bf16[2,224,768]{2,1,0:T(8,128)(2,1)}, bf16[2,224,768]{2,1,0:T(8,128)(2,1)}, u32[]{:S(2)}, u32[]{:S(2)}) %collective-permute-start.7) | collective-permute-done | bytes 688160 | tf_op jit(solution)/shard_map/ppermute | solution.py:596
  70.2 6.7 %project.1 = (bf16[1280,768]{1,0:T(8,128)(2,1)S(1)}, bf16[1280,768]{1,0:T(8,128)(2,1)S(1)}, bf16[1280,768]{1,0:T(8,128)(2,1)S(1)}, bf16[2304,768]{1,0:T(8,128)(2,1)S(1)}) custom-call(s32[2]{0:T(128)S(1)} %pad_add_fusion.place_ref, bf16[256,768]{1,0:T(8,128)(2,1)S(1)} %copy-done.46, bf16[768,768]{1,0:T(8,128)(2,1)S(1)} %copy-done.6, ...), custom_call_target="tpu_custom_call" | custom-call | flops 200000000 | bytes 700000 | tf_op jit(solution)/shard_map/project/pallas_call | solution.py:287
  79.7 5.1 %attend_forward.2 = bf16[384,768]{1,0:T(8,128)(2,1)S(1)} custom-call(s32[3,20]{1,0:T(4,128)S(1)} %get-tuple-element.130.tiles_ref, s32[1,1280]{1,0:T(1,128)S(1)} %get-tuple-element.131.lo_ref, s32[1,1280]{1,0:T(1,128)S(1)} %get-tuple-element.132.hi_ref, bf16[1280,768]{1,0:T(8,128)(2,1)S(1)} %get-tuple-element.164.q_ref, ...), custom_call_target="tpu_custom_call" | custom-call | flops 140000000 | bytes 490000 | tf_op jit(solution)/shard_map/attend_forward/pallas_call | solution.py:190
  85.7 5.3 %collective-permute-done.14.refs_1_ = bf16[2,3,64,768]{3,2,1,0:T(8,128)(2,1)S(1)} collective-permute-done((bf16[2,3,64,768]{3,2,1,0:T(8,128)(2,1)S(1)}, bf16[2,3,64,768]{3,2,1,0:T(8,128)(2,1)S(1)}, u32[]{:S(2)}, u32[]{:S(2)}) %collective-permute-start.14) | collective-permute-done | bytes 589856 | tf_op jit(solution)/shard_map/ppermute | solution.py:630
  100.6 5.9 %attend_forward.3 = bf16[384,768]{1,0:T(8,128)(2,1)S(1)} custom-call(s32[3,20]{1,0:T(4,128)S(1)} %get-tuple-element.130.tiles_ref, s32[1,1280]{1,0:T(1,128)S(1)} %get-tuple-element.131.lo_ref, s32[1,1280]{1,0:T(1,128)S(1)} %get-tuple-element.132.hi_ref, bf16[1280,768]{1,0:T(8,128)(2,1)S(1)} %get-tuple-element.164.q_ref, bf16[1280,768]{1,0:T(8,128)(2,1)S(1)} %copy-done.1, ...), custom_call_target="tpu_custom_call" | custom-call | flops 140000000 | bytes 490000 | tf_op jit(solution)/shard_map/attend_forward/pallas_call | solution.py:190
  124.9 10.8 %fusion.4 = (bf16[768,3072]{1,0:T(8,128)(2,1)}, bf16[768,3072]{1,0:T(8,128)(2,1)S(1)}) fusion(f32[3072]{0:T(1024)S(1)} %bitcast.258, bf16[768,768]{1,0:T(8,128)(2,1)} %fusion.17, bf16[3072,768]{1,0:T(8,128)(2,1)} %copy-done.56), kind=kOutput, calls=%fused_computation.5 | convolution fusion | flops 3652190208 | bytes 15347712 | tf_op jit(solution)/shard_map/dot_general | solution.py:33
  147.1 4.6 %collective-permute-start.24 = (bf16[32,768]{1,0:T(8,128)(2,1)S(1)}, bf16[32,768]{1,0:T(8,128)(2,1)S(1)}, u32[]{:S(2)}, u32[]{:S(2)}) collective-permute-start(bf16[32,768]{1,0:T(8,128)(2,1)S(1)} %fusion.46), channel_id=1, source_target_pairs={{0,3},{1,2},{2,1},{3,0},{4,7},{5,6},{6,5},{7,4},{8,11},{9,10},{10,... | collective-permute-start | bytes 147464 | tf_op jit(solution)/shard_map/ppermute | solution.py:596
  162.7 5.3 %collective-permute-done.27 = bf16[4,32,768]{2,1,0:T(8,128)(2,1)} collective-permute-done((bf16[4,32,768]{2,1,0:T(8,128)(2,1)S(1)}, bf16[4,32,768]{2,1,0:T(8,128)(2,1)}, u32[]{:S(2)}, u32[]{:S(2)}) %collective-permute-start.27) | collective-permute-done | bytes 196640 | tf_op jit(solution)/shard_map/ppermute | solution.py:616
  181.5 7.3 %convert_reduce_fusion = (f32[3072]{0:T(1024)S(1)}, bf16[768,3072]{1,0:T(8,128)(2,1)}) fusion(bf16[768,3072]{1,0:T(8,128)(2,1)} %get-tuple-element.176, bf16[768,768]{1,0:T(8,128)(2,1)S(1)} %convert_element_type.264, bf16[3072,768]{1,0:T(8,128)(2,1)S(1)} %bitcast.231), kind=kOutput, calls=%fused_computation.6 | convolution fusion | flops 3635672064 | bytes 15347712 | tf_op jit(solution)/shard_map/dot_general | solution.py:33
  196.9 6.7 %multiply_reduce_fusion = (f32[768]{0:T(1024)S(1)}, f32[768]{0:T(1024)S(1)}, f32[768]{0:T(1024)S(1)}, f32[768]{0:T(1024)S(1)}, f32[768,768]{1,0:T(8,128)S(1)}) fusion(f32[768,768]{1,0:T(8,128)S(1)} %copy-done.61, f32[768]{0:T(1024)S(1)} %add_rsqrt_fusion.1, f32[768]{0:T(1024)S(1)} %broadcast_multiply_fusion.5, f32[768]{0:T(1024)S(1)} %copy-done.69, ...), kind=kOutput, calls=%fused_computation.23 | convolution fusion | flops 3629773824 | bytes 16536576 | tf_op jit(solution)/shard_map/dot_general | solution.py:33
  220.2 16.1 %attend_backward.2 = (bf16[640,768]{1,0:T(8,128)(2,1)S(1)}, f32[1280,768]{1,0:T(8,128)S(1)}, f32[1280,768]{1,0:T(8,128)S(1)}) custom-call(s32[3,20]{1,0:T(4,128)S(1)} %get-tuple-element.130.tiles_ref, s32[1,1280]{1,0:T(1,128)S(1)} %get-tuple-element.131.lo_ref, s32[1,1280]{1,0:T(1,128)S(1)} %get-tuple-element.132.hi_ref, ...), custom_call_target="tpu_custom_call" | custom-call | flops 320000000 | bytes 1120000 | tf_op jit(solution)/shard_map/attend_backward/pallas_call | solution.py:190
  236.3 6.5 %collective-permute-done.33 = bf16[2,4,96,768]{3,2,1,0:T(8,128)(2,1)S(1)} collective-permute-done((bf16[2,4,96,768]{3,2,1,0:T(8,128)(2,1)S(1)}, bf16[2,4,96,768]{3,2,1,0:T(8,128)(2,1)S(1)}, u32[]{:S(2)}, u32[]{:S(2)}) %collective-permute-start.33) | collective-permute-done | bytes 1179680 | tf_op jit(solution)/shard_map/ppermute | solution.py:630
  242.9 8.4 %collective-permute-done.35 = bf16[2,4,32,768]{3,2,1,0:T(8,128)(2,1)S(1)} collective-permute-done((bf16[2,4,32,768]{3,2,1,0:T(8,128)(2,1)S(1)}, bf16[2,4,32,768]{3,2,1,0:T(8,128)(2,1)S(1)}, u32[]{:S(2)}, u32[]{:S(2)}) %collective-permute-start.35) | collective-permute-done | bytes 393248 | tf_op jit(solution)/shard_map/ppermute | solution.py:630
  252.1 6.2 %attend_backward.3 = (bf16[128,768]{1,0:T(8,128)(2,1)S(1)}, bf16[768,768]{1,0:T(8,128)(2,1)S(1)}, bf16[768,768]{1,0:T(8,128)(2,1)S(1)}) custom-call(s32[3,20]{1,0:T(4,128)S(1)} %get-tuple-element.130.tiles_ref, s32[1,1280]{1,0:T(1,128)S(1)} %get-tuple-element.131.lo_ref, s32[1,1280]{1,0:T(1,128)S(1)} %get-tuple-element.132.hi_ref, ...), custom_call_target="tpu_custom_call" | custom-call | flops 320000000 | bytes 1120000 | tf_op jit(solution)/shard_map/attend_backward/pallas_call | solution.py:190
  258.2 4.8 %piece_grads.1 = (bf16[16,80,768]{2,1,0:T(8,128)(2,1)S(1)}, bf16[16,80,768]{2,1,0:T(8,128)(2,1)S(1)}) custom-call(s32[2]{0:T(128)S(1)} %pad_add_fusion.place_ref, bf16[640,768]{1,0:T(8,128)(2,1)S(1)} %get-tuple-element.183.dq_first_ref, bf16[128,768]{1,0:T(8,128)(2,1)S(1)} %get-tuple-element.191.dq_second_ref, ...), custom_call_target="tpu_custom_call" | custom-call | flops 160000000 | bytes 560000 | tf_op jit(solution)/shard_map/piece_grads/pallas_call | solution.py:287
  264.8 5.7 %collective-permute-start.36 = (bf16[4,96,768]{2,1,0:T(8,128)(2,1)S(1)}, bf16[4,96,768]{2,1,0:T(8,128)(2,1)S(1)}, u32[]{:S(2)}, u32[]{:S(2)}) collective-permute-start(bf16[4,96,768]{2,1,0:T(8,128)(2,1)S(1)} %get-tuple-element.252), channel_id=1, source_target_pairs={{0,8},{4,12},{8,0},{12,4},{16,24},{20,28},{24,16},{28,20},{1,9},{5... | collective-permute-start | bytes 1769480 | tf_op jit(solution)/shard_map/ppermute | solution.py:630
  271.2 17.2 %collective-permute-done.38 = bf16[4,32,768]{2,1,0:T(8,128)(2,1)S(1)} collective-permute-done((bf16[4,32,768]{2,1,0:T(8,128)(2,1)S(1)}, bf16[4,32,768]{2,1,0:T(8,128)(2,1)S(1)}, u32[]{:S(2)}, u32[]{:S(2)}) %collective-permute-start.38) | collective-permute-done | bytes 196640 | tf_op jit(solution)/shard_map/ppermute | solution.py:630
  291.6 13.9 %collective-permute-done.52 = bf16[2,224,768]{2,1,0:T(8,128)(2,1)S(1)} collective-permute-done((bf16[2,224,768]{2,1,0:T(8,128)(2,1)S(1)}, bf16[2,224,768]{2,1,0:T(8,128)(2,1)S(1)}, u32[]{:S(2)}, u32[]{:S(2)}) %collective-permute-start.52) | collective-permute-done | bytes 688160 | tf_op jit(solution)/shard_map/ppermute | solution.py:596
  307.5 4.3 %collective-permute-done.44 = bf16[2,80,768]{2,1,0:T(8,128)(2,1)S(1)} collective-permute-done((bf16[2,80,768]{2,1,0:T(8,128)(2,1)S(1)}, bf16[2,80,768]{2,1,0:T(8,128)(2,1)S(1)}, u32[]{:S(2)}, u32[]{:S(2)}) %collective-permute-start.44) | collective-permute-done | bytes 245792 | tf_op jit(solution)/shard_map/ppermute | solution.py:630
  314.9 16.1 %collective-permute-done.53 = bf16[224,768]{1,0:T(8,128)(2,1)S(1)} collective-permute-done((bf16[224,768]{1,0:T(8,128)(2,1)S(1)}, bf16[224,768]{1,0:T(8,128)(2,1)S(1)}, u32[]{:S(2)}, u32[]{:S(2)}) %collective-permute-start.53) | collective-permute-done | bytes 344096 | tf_op jit(solution)/shard_map/ppermute | solution.py:596
  339.3 5.0 %collective-permute-done.57 = bf16[2,1,112,768]{3,2,0,1:T(8,128)(2,1)S(1)} collective-permute-done((bf16[2,1,112,768]{3,2,0,1:T(8,128)(2,1)S(1)}, bf16[2,1,112,768]{3,2,0,1:T(8,128)(2,1)S(1)}, u32[]{:S(2)}, u32[]{:S(2)}) %collective-permute-start.57) | collective-permute-done | bytes 344096 | tf_op jit(solution)/shard_map/ppermute | solution.py:630
  (425 shorter events, 168.2 us)
Async XLA Ops:
  24.0 17.9 %collective-permute-start.6 = (bf16[1,224,768]{2,1,0:T(8,128)(2,1)S(1)}, bf16[1,224,768]{2,1,0:T(8,128)(2,1)S(1)}, u32[]{:S(2)}, u32[]{:S(2)}) collective-permute-start(bf16[1,224,768]{2,1,0:T(8,128)(2,1)S(1)} %bitcast.267), channel_id=1, source_target_pairs={{0,2},{1,3},{2,0},{3,1},{4,6},{5,7},{6,4},{7,5},{8,10},{9,11},{10,... | collective-permute-start | bytes 1032200 | tf_op jit(solution)/shard_map/ppermute | solution.py:596
  24.1 18.8 %collective-permute-start.8 = (bf16[256,768]{1,0:T(8,128)(2,1)S(1)}, bf16[256,768]{1,0:T(8,128)(2,1)S(1)}, u32[]{:S(2)}, u32[]{:S(2)}) collective-permute-start(bf16[256,768]{1,0:T(8,128)(2,1)S(1)} %get-tuple-element.256), channel_id=1, source_target_pairs={{1,0},{2,1},{3,2},{5,4},{6,5},{7,6},{9,8},{10,9},{11,10},{13,12},{... | collective-permute-start | bytes 1179656 | tf_op jit(solution)/shard_map/ppermute | solution.py:602
  25.4 18.3 %collective-permute-start.5 = (bf16[256,768]{1,0:T(8,128)(2,1)S(1)}, bf16[256,768]{1,0:T(8,128)(2,1)S(1)}, u32[]{:S(2)}, u32[]{:S(2)}) collective-permute-start(bf16[256,768]{1,0:T(8,128)(2,1)S(1)} %get-tuple-element.257), channel_id=1, source_target_pairs={{0,1},{1,2},{2,3},{4,5},{5,6},{6,7},{8,9},{9,10},{10,11},{12,13},{... | collective-permute-start | bytes 1179656 | tf_op jit(solution)/shard_map/ppermute | solution.py:601
  42.9 16.7 %collective-permute-start.7 = (bf16[2,224,768]{2,1,0:T(8,128)(2,1)}, bf16[2,224,768]{2,1,0:T(8,128)(2,1)}, u32[]{:S(2)}, u32[]{:S(2)}) collective-permute-start(bf16[2,224,768]{2,1,0:T(8,128)(2,1)} %pad_maximum_fusion.7), channel_id=1, source_target_pairs={{0,1},{1,0},{2,3},{3,2},{4,5},{5,4},{6,7},{7,6},{8,9},{9,8},{10,11... | collective-permute-start | bytes 2064392 | tf_op jit(solution)/shard_map/ppermute | solution.py:596
  77.0 14.0 %collective-permute-start.14 = (bf16[2,3,64,768]{3,2,1,0:T(8,128)(2,1)S(1)}, bf16[2,3,64,768]{3,2,1,0:T(8,128)(2,1)S(1)}, u32[]{:S(2)}, u32[]{:S(2)}) collective-permute-start(bf16[2,3,64,768]{3,2,1,0:T(8,128)(2,1)S(1)} %get-tuple-element.267.refs_0_), channel_id=1, source_target_pairs={{0,16},{4,20},{8,24},{12,28},{16,0},{20,4},{24,8},{28,12},{1,17},{... | collective-permute-start | bytes 1769480 | tf_op jit(solution)/shard_map/ppermute | solution.py:630
  78.4 13.7 %collective-permute-start.15 = (bf16[2,3,64,768]{3,2,1,0:T(8,128)(2,1)S(1)}, bf16[2,3,64,768]{3,2,1,0:T(8,128)(2,1)S(1)}, u32[]{:S(2)}, u32[]{:S(2)}) collective-permute-start(bf16[2,3,64,768]{3,2,1,0:T(8,128)(2,1)S(1)} %get-tuple-element.269.refs_2_), channel_id=1, source_target_pairs={{0,8},{4,12},{8,0},{12,4},{16,24},{20,28},{24,16},{28,20},{1,9},{5... | collective-permute-start | bytes 1769480 | tf_op jit(solution)/shard_map/ppermute | solution.py:630
  93.8 16.0 %collective-permute-start.16 = (bf16[4,2,3,64,768]{4,3,2,1,0:T(8,128)(2,1)}, bf16[4,2,3,64,768]{4,3,2,1,0:T(8,128)(2,1)}, u32[]{:S(2)}, u32[]{:S(2)}) collective-permute-start(bf16[4,2,3,64,768]{4,3,2,1,0:T(8,128)(2,1)} %pad_maximum_fusion), channel_id=1, source_target_pairs={{0,4},{4,0},{8,12},{12,8},{16,20},{20,16},{24,28},{28,24},{1,5},{5... | collective-permute-start | bytes 7077896 | tf_op jit(solution)/shard_map/ppermute | solution.py:630
  179.4 13.5 %collective-permute-start.28 = (bf16[1536,768]{1,0:T(8,128)(2,1)S(1)}, bf16[1536,768]{1,0:T(8,128)(2,1)S(1)}, u32[]{:S(2)}, u32[]{:S(2)}) collective-permute-start(bf16[1536,768]{1,0:T(8,128)(2,1)S(1)} %convolution_convert_fusion.1), channel_id=1, source_target_pairs={{0,4},{4,0},{8,12},{12,8},{16,20},{20,16},{24,28},{28,24},{1,5},{5... | collective-permute-start | bytes 7077896 | tf_op jit(solution)/shard_map/ppermute | solution.py:630
  192.7 20.3 %collective-permute-start.31 = (bf16[1536,768]{1,0:T(8,128)(2,1)S(1)}, bf16[1536,768]{1,0:T(8,128)(2,1)S(1)}, u32[]{:S(2)}, u32[]{:S(2)}) collective-permute-start(bf16[1536,768]{1,0:T(8,128)(2,1)S(1)} %convolution_convert_fusion), channel_id=1, source_target_pairs={{0,4},{4,0},{8,12},{12,8},{16,20},{20,16},{24,28},{28,24},{1,5},{5... | collective-permute-start | bytes 7077896 | tf_op jit(solution)/shard_map/ppermute | solution.py:630
  215.2 27.6 %collective-permute-start.33 = (bf16[2,4,96,768]{3,2,1,0:T(8,128)(2,1)S(1)}, bf16[2,4,96,768]{3,2,1,0:T(8,128)(2,1)S(1)}, u32[]{:S(2)}, u32[]{:S(2)}) collective-permute-start(bf16[2,4,96,768]{3,2,1,0:T(8,128)(2,1)S(1)} %slice_bitcast_fusion.1), channel_id=1, source_target_pairs={{0,8},{4,12},{8,0},{12,4},{16,24},{20,28},{24,16},{28,20},{1,9},{5... | collective-permute-start | bytes 3538952 | tf_op jit(solution)/shard_map/ppermute | solution.py:630
  215.5 27.4 %collective-permute-start.32 = (bf16[2,4,96,768]{3,2,1,0:T(8,128)(2,1)S(1)}, bf16[2,4,96,768]{3,2,1,0:T(8,128)(2,1)S(1)}, u32[]{:S(2)}, u32[]{:S(2)}) collective-permute-start(bf16[2,4,96,768]{3,2,1,0:T(8,128)(2,1)S(1)} %bitcast.269), channel_id=1, source_target_pairs={{0,16},{4,20},{8,24},{12,28},{16,0},{20,4},{24,8},{28,12},{1,17},{... | collective-permute-start | bytes 3538952 | tf_op jit(solution)/shard_map/ppermute | solution.py:630
  218.1 33.1 %collective-permute-start.35 = (bf16[2,4,32,768]{3,2,1,0:T(8,128)(2,1)S(1)}, bf16[2,4,32,768]{3,2,1,0:T(8,128)(2,1)S(1)}, u32[]{:S(2)}, u32[]{:S(2)}) collective-permute-start(bf16[2,4,32,768]{3,2,1,0:T(8,128)(2,1)S(1)} %bitcast.270), channel_id=1, source_target_pairs={{0,16},{4,20},{8,24},{12,28},{16,0},{20,4},{24,8},{28,12},{1,17},{... | collective-permute-start | bytes 1179656 | tf_op jit(solution)/shard_map/ppermute | solution.py:630
  263.0 26.0 %collective-permute-start.39 = (bf16[16,80,768]{2,1,0:T(8,128)(2,1)S(1)}, bf16[16,80,768]{2,1,0:T(8,128)(2,1)S(1)}, u32[]{:S(2)}, u32[]{:S(2)}) collective-permute-start(bf16[16,80,768]{2,1,0:T(8,128)(2,1)S(1)} %get-tuple-element.203), channel_id=1, source_target_pairs={{0,4},{4,0},{8,12},{12,8},{16,20},{20,16},{24,28},{28,24},{1,5},{5... | collective-permute-start | bytes 5898248 | tf_op jit(solution)/shard_map/ppermute | solution.py:630
  264.8 23.6 %collective-permute-start.36 = (bf16[4,96,768]{2,1,0:T(8,128)(2,1)S(1)}, bf16[4,96,768]{2,1,0:T(8,128)(2,1)S(1)}, u32[]{:S(2)}, u32[]{:S(2)}) collective-permute-start(bf16[4,96,768]{2,1,0:T(8,128)(2,1)S(1)} %get-tuple-element.252), channel_id=1, source_target_pairs={{0,8},{4,12},{8,0},{12,4},{16,24},{20,28},{24,16},{28,20},{1,9},{5... | collective-permute-start | bytes 1769480 | tf_op jit(solution)/shard_map/ppermute | solution.py:630
  270.5 17.9 %collective-permute-start.37 = (bf16[4,96,768]{2,1,0:T(8,128)(2,1)S(1)}, bf16[4,96,768]{2,1,0:T(8,128)(2,1)S(1)}, u32[]{:S(2)}, u32[]{:S(2)}) collective-permute-start(bf16[4,96,768]{2,1,0:T(8,128)(2,1)S(1)} %get-tuple-element.250), channel_id=1, source_target_pairs={{0,16},{4,20},{8,24},{12,28},{16,0},{20,4},{24,8},{28,12},{1,17},{... | collective-permute-start | bytes 1769480 | tf_op jit(solution)/shard_map/ppermute | solution.py:630
  271.0 17.4 %collective-permute-start.38 = (bf16[4,32,768]{2,1,0:T(8,128)(2,1)S(1)}, bf16[4,32,768]{2,1,0:T(8,128)(2,1)S(1)}, u32[]{:S(2)}, u32[]{:S(2)}) collective-permute-start(bf16[4,32,768]{2,1,0:T(8,128)(2,1)S(1)} %get-tuple-element.278), channel_id=1, source_target_pairs={{0,8},{4,12},{8,0},{12,4},{16,24},{20,28},{24,16},{28,20},{1,9},{5... | collective-permute-start | bytes 589832 | tf_op jit(solution)/shard_map/ppermute | solution.py:630
  289.0 16.5 %collective-permute-start.52 = (bf16[2,224,768]{2,1,0:T(8,128)(2,1)S(1)}, bf16[2,224,768]{2,1,0:T(8,128)(2,1)S(1)}, u32[]{:S(2)}, u32[]{:S(2)}) collective-permute-start(bf16[2,224,768]{2,1,0:T(8,128)(2,1)S(1)} %pad_maximum_fusion.8), channel_id=1, source_target_pairs={{0,1},{1,0},{2,3},{3,2},{4,5},{5,4},{6,7},{7,6},{8,9},{9,8},{10,11... | collective-permute-start | bytes 2064392 | tf_op jit(solution)/shard_map/ppermute | solution.py:596
  289.7 15.7 %collective-permute-start.43 = (bf16[2,2,80,768]{3,2,1,0:T(8,128)(2,1)S(1)}, bf16[2,2,80,768]{3,2,1,0:T(8,128)(2,1)S(1)}, u32[]{:S(2)}, u32[]{:S(2)}) collective-permute-start(bf16[2,2,80,768]{3,2,1,0:T(8,128)(2,1)S(1)} %slice_bitcast_fusion.6), channel_id=1, source_target_pairs={{0,8},{4,12},{8,0},{12,4},{16,24},{20,28},{24,16},{28,20},{1,9},{5... | collective-permute-start | bytes 1474568 | tf_op jit(solution)/shard_map/ppermute | solution.py:630
  291.1 14.4 %collective-permute-start.40 = (bf16[2,2,80,768]{3,2,1,0:T(8,128)(2,1)S(1)}, bf16[2,2,80,768]{3,2,1,0:T(8,128)(2,1)S(1)}, u32[]{:S(2)}, u32[]{:S(2)}) collective-permute-start(bf16[2,2,80,768]{3,2,1,0:T(8,128)(2,1)S(1)} %slice_bitcast_fusion.8), channel_id=1, source_target_pairs={{0,16},{4,20},{8,24},{12,28},{16,0},{20,4},{24,8},{28,12},{1,17},{... | collective-permute-start | bytes 1474568 | tf_op jit(solution)/shard_map/ppermute | solution.py:630
  307.5 23.5 %collective-permute-start.53 = (bf16[224,768]{1,0:T(8,128)(2,1)S(1)}, bf16[224,768]{1,0:T(8,128)(2,1)S(1)}, u32[]{:S(2)}, u32[]{:S(2)}) collective-permute-start(bf16[224,768]{1,0:T(8,128)(2,1)S(1)} %fusion.35), channel_id=1, source_target_pairs={{0,2},{1,3},{2,0},{3,1},{4,6},{5,7},{6,4},{7,5},{8,10},{9,11},{10,... | collective-permute-start | bytes 1032200 | tf_op jit(solution)/shard_map/ppermute | solution.py:596
  311.9 21.7 %collective-permute-start.45 = (bf16[80,768]{1,0:T(8,128)(2,1)S(1)}, bf16[80,768]{1,0:T(8,128)(2,1)S(1)}, u32[]{:S(2)}, u32[]{:S(2)}) collective-permute-start(bf16[80,768]{1,0:T(8,128)(2,1)S(1)} %get-tuple-element.298), channel_id=1, source_target_pairs={{0,2},{1,3},{2,0},{3,1},{4,6},{5,7},{6,4},{7,5},{8,10},{9,11},{10,... | collective-permute-start | bytes 368648 | tf_op jit(solution)/shard_map/ppermute | solution.py:596
  312.0 21.6 %collective-permute-start.46 = (bf16[80,768]{1,0:T(8,128)(2,1)S(1)}, bf16[80,768]{1,0:T(8,128)(2,1)S(1)}, u32[]{:S(2)}, u32[]{:S(2)}) collective-permute-start(bf16[80,768]{1,0:T(8,128)(2,1)S(1)} %get-tuple-element.299), channel_id=1, source_target_pairs={{0,3},{1,2},{2,1},{3,0},{4,7},{5,6},{6,5},{7,4},{8,11},{9,10},{10,... | collective-permute-start | bytes 368648 | tf_op jit(solution)/shard_map/ppermute | solution.py:596
  314.8 18.8 %collective-permute-start.42 = (bf16[80,768]{1,0:T(8,128)(2,1)S(1)}, bf16[80,768]{1,0:T(8,128)(2,1)S(1)}, u32[]{:S(2)}, u32[]{:S(2)}) collective-permute-start(bf16[80,768]{1,0:T(8,128)(2,1)S(1)} %slice_bitcast_fusion.22), channel_id=1, source_target_pairs={{0,1},{1,0},{2,3},{3,2},{4,5},{5,4},{6,7},{7,6},{8,9},{9,8},{10,11... | collective-permute-start | bytes 368648 | tf_op jit(solution)/shard_map/ppermute | solution.py:596
  344.7 14.9 %collective-permute-start.58 = (bf16[4,2,1,112,768]{4,3,2,1,0:T(8,128)(2,1)S(1)}, bf16[4,2,1,112,768]{4,3,2,1,0:T(8,128)(2,1)S(1)}, u32[]{:S(2)}, u32[]{:S(2)}) collective-permute-start(bf16[4,2,1,112,768]{4,3,2,1,0:T(8,128)(2,1)S(1)} %pad_maximum_fusion.4), channel_id=1, source_target_pairs={{0,4},{4,0},{8,12},{12,8},{16,20},{20,16},{24,28},{28,24},{1,5},{5... | collective-permute-start | bytes 4128776 | tf_op jit(solution)/shard_map/ppermute | solution.py:630
  (119 other events, 777.6 us)

commit v2 on v1

--- a/solution.py
+++ b/solution.py
@@ -904,8 +904,8 @@
     early_halves = [(back_sum[0], back_half), (in_sum[0], in_half), (out_sum[0], out_half)]
     early_halves = after(early_halves, late_query)
     early_sum = jnp.concatenate([add(*half) for half in early_halves], axis=1)
+    tokens_low, early_sum = lax.optimization_barrier((tokens, early_sum))
     early_parts = [early_sum[i] for i in range(ways)]
-    tokens_low = after(tokens, early_parts)
 
     late_rows = 3 * part + 8
     late_keep, late_sent = local(

time: 369 us -> 358 us (0.970)
  waiting for transfers between devices: 134 us -> 118 us
  Pallas kernels: 63.6 us -> 68.8 us
    ppermute x39, waiting for transfers between devices: 61.6 us -> 49.7 us  [swap(): return lax.ppermute(values, 'dp', [(i, i ^ bit) for i in range(ways)])]
    pallas_call x4, Pallas kernels: 33.2 us -> 38.5 us  [attention(): pl.pallas_call(kernel, out_shape=tuple((jax.ShapeDtypeStruct(shape, dtype...]
  transfers between devices with their start and end apart: 59 -> 59, of which waited for: 29 -> 30; matrix products, arithmetic and copies ran while one was open for 15% -> 15% of each run, Pallas kernels for 12% -> 16%
where the time goes in v2:
time: 358 us; the launch traced here: 353 us
  waiting for transfers between devices  118 us (33%)
  Pallas kernels  68.8 us (19%)
  starting transfers between devices  66.7 us (19%)
  matrix products  54 us (15%)
  local copies, waits for them, and re-layouts  24.9 us (7%)
  other arithmetic  17.7 us (5%)
    ppermute x13, waiting for transfers between devices, partner(): return lax.ppermute(values, 'mp', [(i, i ^ step) for i in range(ways)])  58.9 us
    ppermute x39, waiting for transfers between devices, swap(): return lax.ppermute(values, 'dp', [(i, i ^ bit) for i in range(ways)])  49.7 us
    dot_general x15, matrix products, mm(): return lax.dot_general(a, b, dims, preferred_element_type=f32)  49.3 us
    ppermute x39, starting transfers between devices, swap(): return lax.ppermute(values, 'dp', [(i, i ^ bit) for i in range(ways)])  39.7 us
    pallas_call x4, Pallas kernels, attention(): pl.pallas_call(kernel, out_shape=tuple((jax.ShapeDtypeStruct(shape, dtype...  38.5 us
    pallas_call x11, Pallas kernels, local(): pl.pallas_call(kernel, out_shape=tuple((jax.ShapeDtypeStruct(shape, dtype...  28.1 us
    unnamed x168, local copies, waits for them, and re-layouts  15.9 us
    ppermute x13, starting transfers between devices, partner(): return lax.ppermute(values, 'mp', [(i, i ^ step) for i in range(ways)])  13.7 us
  transfers between devices with their start and end apart: 59, of which 30 were waited for; matrix products, arithmetic and copies ran while one was open for 15% of the time, Pallas kernels for 16%

profile of v2, /device:TPU:1, one launch (start us, length us, event | category | flops | bytes accessed | tf_op | source)
XLA Modules:
  0.0 352.7 jit_solution(10512978660713104061)
XLA Ops:
  7.1 4.2 %collective-permute-start.2 = (bf16[80,768]{1,0:T(8,128)(2,1)S(1)}, bf16[80,768]{1,0:T(8,128)(2,1)S(1)}, u32[]{:S(2)}, u32[]{:S(2)}) collective-permute-start(bf16[80,768]{1,0:T(8,128)(2,1)S(1)} %fusion.42), channel_id=1, source_target_pairs={{0,3},{1,2},{2,1},{3,0},{4,7},{5,6},{6,5},{7,4},{8,11},{9,10},{10,... | collective-permute-start | bytes 368648 | tf_op jit(solution)/shard_map/ppermute | solution.py:596
  14.4 6.9 %collective-permute-done.1 = bf16[80,768]{1,0:T(8,128)(2,1)S(1)} collective-permute-done((bf16[80,768]{1,0:T(8,128)(2,1)S(1)}, bf16[80,768]{1,0:T(8,128)(2,1)S(1)}, u32[]{:S(2)}, u32[]{:S(2)}) %collective-permute-start.1) | collective-permute-done | bytes 122912 | tf_op jit(solution)/shard_map/ppermute | solution.py:596
  25.4 4.8 %collective-permute-start.5 = (bf16[256,768]{1,0:T(8,128)(2,1)S(1)}, bf16[256,768]{1,0:T(8,128)(2,1)S(1)}, u32[]{:S(2)}, u32[]{:S(2)}) collective-permute-start(bf16[256,768]{1,0:T(8,128)(2,1)S(1)} %get-tuple-element.259), channel_id=1, source_target_pairs={{0,1},{1,2},{2,3},{4,5},{5,6},{6,7},{8,9},{9,10},{10,11},{12,13},{... | collective-permute-start | bytes 1179656 | tf_op jit(solution)/shard_map/ppermute | solution.py:601
  30.3 11.6 %collective-permute-done.6 = bf16[1,224,768]{2,1,0:T(8,128)(2,1)S(1)} collective-permute-done((bf16[1,224,768]{2,1,0:T(8,128)(2,1)S(1)}, bf16[1,224,768]{2,1,0:T(8,128)(2,1)S(1)}, u32[]{:S(2)}, u32[]{:S(2)}) %collective-permute-start.6) | collective-permute-done | bytes 344096 | tf_op jit(solution)/shard_map/ppermute | solution.py:596
  51.9 7.7 %collective-permute-done.7 = bf16[2,224,768]{2,1,0:T(8,128)(2,1)} collective-permute-done((bf16[2,224,768]{2,1,0:T(8,128)(2,1)}, bf16[2,224,768]{2,1,0:T(8,128)(2,1)}, u32[]{:S(2)}, u32[]{:S(2)}) %collective-permute-start.7) | collective-permute-done | bytes 688160 | tf_op jit(solution)/shard_map/ppermute | solution.py:596
  70.2 6.7 %project.1 = (bf16[1280,768]{1,0:T(8,128)(2,1)S(1)}, bf16[1280,768]{1,0:T(8,128)(2,1)S(1)}, bf16[1280,768]{1,0:T(8,128)(2,1)S(1)}, bf16[2304,768]{1,0:T(8,128)(2,1)S(1)}) custom-call(s32[2]{0:T(128)S(1)} %pad_add_fusion.place_ref, bf16[256,768]{1,0:T(8,128)(2,1)S(1)} %copy-done.46, bf16[768,768]{1,0:T(8,128)(2,1)S(1)} %copy-done.6, ...), custom_call_target="tpu_custom_call" | custom-call | flops 200000000 | bytes 700000 | tf_op jit(solution)/shard_map/project/pallas_call | solution.py:287
  79.7 5.1 %attend_forward.2 = bf16[384,768]{1,0:T(8,128)(2,1)S(1)} custom-call(s32[3,20]{1,0:T(4,128)S(1)} %get-tuple-element.131.tiles_ref, s32[1,1280]{1,0:T(1,128)S(1)} %get-tuple-element.132.lo_ref, s32[1,1280]{1,0:T(1,128)S(1)} %get-tuple-element.133.hi_ref, bf16[1280,768]{1,0:T(8,128)(2,1)S(1)} %get-tuple-element.165.q_ref, ...), custom_call_target="tpu_custom_call" | custom-call | flops 140000000 | bytes 490000 | tf_op jit(solution)/shard_map/attend_forward/pallas_call | solution.py:190
  85.7 5.3 %collective-permute-done.14.refs_1_ = bf16[2,3,64,768]{3,2,1,0:T(8,128)(2,1)S(1)} collective-permute-done((bf16[2,3,64,768]{3,2,1,0:T(8,128)(2,1)S(1)}, bf16[2,3,64,768]{3,2,1,0:T(8,128)(2,1)S(1)}, u32[]{:S(2)}, u32[]{:S(2)}) %collective-permute-start.14) | collective-permute-done | bytes 589856 | tf_op jit(solution)/shard_map/ppermute | solution.py:630
  100.6 6.3 %attend_forward.3 = bf16[384,768]{1,0:T(8,128)(2,1)S(1)} custom-call(s32[3,20]{1,0:T(4,128)S(1)} %get-tuple-element.131.tiles_ref, s32[1,1280]{1,0:T(1,128)S(1)} %get-tuple-element.132.lo_ref, s32[1,1280]{1,0:T(1,128)S(1)} %get-tuple-element.133.hi_ref, bf16[1280,768]{1,0:T(8,128)(2,1)S(1)} %get-tuple-element.165.q_ref, bf16[1280,768]{1,0:T(8,128)(2,1)S(1)} %copy-done.1, ...), custom_call_target="tpu_custom_call" | custom-call | flops 140000000 | bytes 490000 | tf_op jit(solution)/shard_map/attend_forward/pallas_call | solution.py:190
  124.7 10.8 %fusion.4 = (bf16[768,3072]{1,0:T(8,128)(2,1)}, bf16[768,3072]{1,0:T(8,128)(2,1)S(1)}) fusion(f32[3072]{0:T(1024)S(1)} %bitcast.253, bf16[768,768]{1,0:T(8,128)(2,1)} %fusion.17, bf16[3072,768]{1,0:T(8,128)(2,1)} %copy-done.56), kind=kOutput, calls=%fused_computation.5 | convolution fusion | flops 3652190208 | bytes 15347712 | tf_op jit(solution)/shard_map/dot_general | solution.py:33
  139.5 4.1 %fusion.84 = (f32[768]{0:T(1024)S(1)}, f32[768,768]{1,0:T(8,128)S(1)}) fusion(f32[768]{0:T(1024)S(1)} %copy-done.73, bf16[768,3072]{1,0:T(8,128)(2,1)S(1)} %get-tuple-element.175, bf16[3072,768]{1,0:T(8,128)(2,1)S(1)} %join_back.1, f32[768]{0:T(1024)S(1)} %copy-done.70, f32[768]{0:T(1024)S(1)} %copy-done.69, f32[768]{0:T(1024)S(1)} %add_rsqrt_fusion.1, ...), kind=kOutput, calls=%fused_computation.224 | convolution fusion | flops 3628006656 | bytes 14174208 | tf_op jit(solution)/shard_map/dot_general | solution.py:33
  162.3 4.6 %collective-permute-done.27 = bf16[4,32,768]{2,1,0:T(8,128)(2,1)} collective-permute-done((bf16[4,32,768]{2,1,0:T(8,128)(2,1)S(1)}, bf16[4,32,768]{2,1,0:T(8,128)(2,1)}, u32[]{:S(2)}, u32[]{:S(2)}) %collective-permute-start.27) | collective-permute-done | bytes 196640 | tf_op jit(solution)/shard_map/ppermute | solution.py:616
  170.7 4.2 %multiply_reduce_fusion.1 = (f32[768]{0:T(1024)S(1)}, f32[768]{0:T(1024)S(1)}, f32[768]{0:T(1024)S(1)}, f32[768]{0:T(1024)S(1)}, f32[768,768]{1,0:T(8,128)S(1)}) fusion(f32[768,768]{1,0:T(8,128)} %copy-done.62, f32[768]{0:T(1024)S(1)} %add_rsqrt_fusion, f32[768]{0:T(1024)S(1)} %broadcast_multiply_fusion.4, f32[768]{0:T(1024)S(1)} %copy-done.68, ...), kind=kOutput, calls=%fused_computation.24 | convolution fusion | flops 176391168 | bytes 5993568 | tf_op jit(solution)/shard_map/dot_general | solution.py:836
  180.5 7.3 %convert_reduce_fusion = (f32[3072]{0:T(1024)S(1)}, bf16[768,3072]{1,0:T(8,128)(2,1)}) fusion(bf16[768,3072]{1,0:T(8,128)(2,1)} %get-tuple-element.177, bf16[768,768]{1,0:T(8,128)(2,1)S(1)} %convert_element_type.269, bf16[3072,768]{1,0:T(8,128)(2,1)S(1)} %bitcast.226), kind=kOutput, calls=%fused_computation.6 | convolution fusion | flops 3635672064 | bytes 15347712 | tf_op jit(solution)/shard_map/dot_general | solution.py:33
  195.8 6.7 %multiply_reduce_fusion = (f32[768]{0:T(1024)S(1)}, f32[768]{0:T(1024)S(1)}, f32[768]{0:T(1024)S(1)}, f32[768]{0:T(1024)S(1)}, f32[768,768]{1,0:T(8,128)S(1)}) fusion(f32[768,768]{1,0:T(8,128)S(1)} %copy-done.61, f32[768]{0:T(1024)S(1)} %add_rsqrt_fusion.1, f32[768]{0:T(1024)S(1)} %broadcast_multiply_fusion.5, f32[768]{0:T(1024)S(1)} %copy-done.69, ...), kind=kOutput, calls=%fused_computation.23 | convolution fusion | flops 3629773824 | bytes 16536576 | tf_op jit(solution)/shard_map/dot_general | solution.py:33
  219.6 16.2 %attend_backward.2 = (bf16[640,768]{1,0:T(8,128)(2,1)S(1)}, f32[1280,768]{1,0:T(8,128)S(1)}, f32[1280,768]{1,0:T(8,128)S(1)}) custom-call(s32[3,20]{1,0:T(4,128)S(1)} %get-tuple-element.131.tiles_ref, s32[1,1280]{1,0:T(1,128)S(1)} %get-tuple-element.132.lo_ref, s32[1,1280]{1,0:T(1,128)S(1)} %get-tuple-element.133.hi_ref, ...), custom_call_target="tpu_custom_call" | custom-call | flops 320000000 | bytes 1120000 | tf_op jit(solution)/shard_map/attend_backward/pallas_call | solution.py:190
  235.9 5.9 %collective-permute-done.33 = bf16[2,4,96,768]{3,2,1,0:T(8,128)(2,1)S(1)} collective-permute-done((bf16[2,4,96,768]{3,2,1,0:T(8,128)(2,1)S(1)}, bf16[2,4,96,768]{3,2,1,0:T(8,128)(2,1)S(1)}, u32[]{:S(2)}, u32[]{:S(2)}) %collective-permute-start.33) | collective-permute-done | bytes 1179680 | tf_op jit(solution)/shard_map/ppermute | solution.py:630
  242.0 8.4 %collective-permute-done.35 = bf16[2,4,32,768]{3,2,1,0:T(8,128)(2,1)S(1)} collective-permute-done((bf16[2,4,32,768]{3,2,1,0:T(8,128)(2,1)S(1)}, bf16[2,4,32,768]{3,2,1,0:T(8,128)(2,1)S(1)}, u32[]{:S(2)}, u32[]{:S(2)}) %collective-permute-start.35) | collective-permute-done | bytes 393248 | tf_op jit(solution)/shard_map/ppermute | solution.py:630
  254.0 10.9 %attend_backward.3 = (bf16[128,768]{1,0:T(8,128)(2,1)S(1)}, bf16[768,768]{1,0:T(8,128)(2,1)S(1)}, bf16[768,768]{1,0:T(8,128)(2,1)S(1)}) custom-call(s32[3,20]{1,0:T(4,128)S(1)} %get-tuple-element.131.tiles_ref, s32[1,1280]{1,0:T(1,128)S(1)} %get-tuple-element.132.lo_ref, s32[1,1280]{1,0:T(1,128)S(1)} %get-tuple-element.133.hi_ref, ...), custom_call_target="tpu_custom_call" | custom-call | flops 320000000 | bytes 1120000 | tf_op jit(solution)/shard_map/attend_backward/pallas_call | solution.py:190
  264.9 4.2 %collective-permute-done.38 = bf16[4,32,768]{2,1,0:T(8,128)(2,1)S(1)} collective-permute-done((bf16[4,32,768]{2,1,0:T(8,128)(2,1)S(1)}, bf16[4,32,768]{2,1,0:T(8,128)(2,1)S(1)}, u32[]{:S(2)}, u32[]{:S(2)}) %collective-permute-start.38) | collective-permute-done | bytes 196640 | tf_op jit(solution)/shard_map/ppermute | solution.py:630
  269.5 4.8 %piece_grads.1 = (bf16[16,80,768]{2,1,0:T(8,128)(2,1)S(1)}, bf16[16,80,768]{2,1,0:T(8,128)(2,1)S(1)}) custom-call(s32[2]{0:T(128)S(1)} %pad_add_fusion.place_ref, bf16[640,768]{1,0:T(8,128)(2,1)S(1)} %get-tuple-element.184.dq_first_ref, bf16[128,768]{1,0:T(8,128)(2,1)S(1)} %get-tuple-element.192.dq_second_ref, ...), custom_call_target="tpu_custom_call" | custom-call | flops 160000000 | bytes 560000 | tf_op jit(solution)/shard_map/piece_grads/pallas_call | solution.py:287
  282.7 11.0 %collective-permute-done.52 = bf16[2,224,768]{2,1,0:T(8,128)(2,1)S(1)} collective-permute-done((bf16[2,224,768]{2,1,0:T(8,128)(2,1)S(1)}, bf16[2,224,768]{2,1,0:T(8,128)(2,1)S(1)}, u32[]{:S(2)}, u32[]{:S(2)}) %collective-permute-start.52) | collective-permute-done | bytes 688160 | tf_op jit(solution)/shard_map/ppermute | solution.py:596
  303.3 16.3 %collective-permute-done.53 = bf16[224,768]{1,0:T(8,128)(2,1)S(1)} collective-permute-done((bf16[224,768]{1,0:T(8,128)(2,1)S(1)}, bf16[224,768]{1,0:T(8,128)(2,1)S(1)}, u32[]{:S(2)}, u32[]{:S(2)}) %collective-permute-start.53) | collective-permute-done | bytes 344096 | tf_op jit(solution)/shard_map/ppermute | solution.py:596
  328.2 4.3 %collective-permute-done.57 = bf16[2,1,112,768]{3,2,0,1:T(8,128)(2,1)S(1)} collective-permute-done((bf16[2,1,112,768]{3,2,0,1:T(8,128)(2,1)S(1)}, bf16[2,1,112,768]{3,2,0,1:T(8,128)(2,1)S(1)}, u32[]{:S(2)}, u32[]{:S(2)}) %collective-permute-start.57) | collective-permute-done | bytes 344096 | tf_op jit(solution)/shard_map/ppermute | solution.py:630
  (425 shorter events, 171.7 us)
Async XLA Ops:
  24.0 17.9 %collective-permute-start.6 = (bf16[1,224,768]{2,1,0:T(8,128)(2,1)S(1)}, bf16[1,224,768]{2,1,0:T(8,128)(2,1)S(1)}, u32[]{:S(2)}, u32[]{:S(2)}) collective-permute-start(bf16[1,224,768]{2,1,0:T(8,128)(2,1)S(1)} %bitcast.262), channel_id=1, source_target_pairs={{0,2},{1,3},{2,0},{3,1},{4,6},{5,7},{6,4},{7,5},{8,10},{9,11},{10,... | collective-permute-start | bytes 1032200 | tf_op jit(solution)/shard_map/ppermute | solution.py:596
  24.1 18.8 %collective-permute-start.8 = (bf16[256,768]{1,0:T(8,128)(2,1)S(1)}, bf16[256,768]{1,0:T(8,128)(2,1)S(1)}, u32[]{:S(2)}, u32[]{:S(2)}) collective-permute-start(bf16[256,768]{1,0:T(8,128)(2,1)S(1)} %get-tuple-element.258), channel_id=1, source_target_pairs={{1,0},{2,1},{3,2},{5,4},{6,5},{7,6},{9,8},{10,9},{11,10},{13,12},{... | collective-permute-start | bytes 1179656 | tf_op jit(solution)/shard_map/ppermute | solution.py:602
  25.4 18.3 %collective-permute-start.5 = (bf16[256,768]{1,0:T(8,128)(2,1)S(1)}, bf16[256,768]{1,0:T(8,128)(2,1)S(1)}, u32[]{:S(2)}, u32[]{:S(2)}) collective-permute-start(bf16[256,768]{1,0:T(8,128)(2,1)S(1)} %get-tuple-element.259), channel_id=1, source_target_pairs={{0,1},{1,2},{2,3},{4,5},{5,6},{6,7},{8,9},{9,10},{10,11},{12,13},{... | collective-permute-start | bytes 1179656 | tf_op jit(solution)/shard_map/ppermute | solution.py:601
  42.9 16.7 %collective-permute-start.7 = (bf16[2,224,768]{2,1,0:T(8,128)(2,1)}, bf16[2,224,768]{2,1,0:T(8,128)(2,1)}, u32[]{:S(2)}, u32[]{:S(2)}) collective-permute-start(bf16[2,224,768]{2,1,0:T(8,128)(2,1)} %pad_maximum_fusion.7), channel_id=1, source_target_pairs={{0,1},{1,0},{2,3},{3,2},{4,5},{5,4},{6,7},{7,6},{8,9},{9,8},{10,11... | collective-permute-start | bytes 2064392 | tf_op jit(solution)/shard_map/ppermute | solution.py:596
  77.0 14.0 %collective-permute-start.14 = (bf16[2,3,64,768]{3,2,1,0:T(8,128)(2,1)S(1)}, bf16[2,3,64,768]{3,2,1,0:T(8,128)(2,1)S(1)}, u32[]{:S(2)}, u32[]{:S(2)}) collective-permute-start(bf16[2,3,64,768]{3,2,1,0:T(8,128)(2,1)S(1)} %get-tuple-element.269.refs_0_), channel_id=1, source_target_pairs={{0,16},{4,20},{8,24},{12,28},{16,0},{20,4},{24,8},{28,12},{1,17},{... | collective-permute-start | bytes 1769480 | tf_op jit(solution)/shard_map/ppermute | solution.py:630
  78.4 13.7 %collective-permute-start.15 = (bf16[2,3,64,768]{3,2,1,0:T(8,128)(2,1)S(1)}, bf16[2,3,64,768]{3,2,1,0:T(8,128)(2,1)S(1)}, u32[]{:S(2)}, u32[]{:S(2)}) collective-permute-start(bf16[2,3,64,768]{3,2,1,0:T(8,128)(2,1)S(1)} %get-tuple-element.271.refs_2_), channel_id=1, source_target_pairs={{0,8},{4,12},{8,0},{12,4},{16,24},{20,28},{24,16},{28,20},{1,9},{5... | collective-permute-start | bytes 1769480 | tf_op jit(solution)/shard_map/ppermute | solution.py:630
  93.8 15.8 %collective-permute-start.16 = (bf16[4,2,3,64,768]{4,3,2,1,0:T(8,128)(2,1)}, bf16[4,2,3,64,768]{4,3,2,1,0:T(8,128)(2,1)}, u32[]{:S(2)}, u32[]{:S(2)}) collective-permute-start(bf16[4,2,3,64,768]{4,3,2,1,0:T(8,128)(2,1)} %pad_maximum_fusion), channel_id=1, source_target_pairs={{0,4},{4,0},{8,12},{12,8},{16,20},{20,16},{24,28},{28,24},{1,5},{5... | collective-permute-start | bytes 7077896 | tf_op jit(solution)/shard_map/ppermute | solution.py:630
  123.0 12.6 %collective-permute-start.21 = (bf16[4,2,3,48,768]{4,3,2,1,0:T(8,128)(2,1)}, bf16[4,2,3,48,768]{4,3,2,1,0:T(8,128)(2,1)}, u32[]{:S(2)}, u32[]{:S(2)}) collective-permute-start(bf16[4,2,3,48,768]{4,3,2,1,0:T(8,128)(2,1)} %pad_maximum_fusion.1), channel_id=1, source_target_pairs={{0,4},{4,0},{8,12},{12,8},{16,20},{20,16},{24,28},{28,24},{1,5},{5... | collective-permute-start | bytes 5308424 | tf_op jit(solution)/shard_map/ppermute | solution.py:630
  178.3 13.5 %collective-permute-start.28 = (bf16[1536,768]{1,0:T(8,128)(2,1)S(1)}, bf16[1536,768]{1,0:T(8,128)(2,1)S(1)}, u32[]{:S(2)}, u32[]{:S(2)}) collective-permute-start(bf16[1536,768]{1,0:T(8,128)(2,1)S(1)} %convolution_convert_fusion.1), channel_id=1, source_target_pairs={{0,4},{4,0},{8,12},{12,8},{16,20},{20,16},{24,28},{28,24},{1,5},{5... | collective-permute-start | bytes 7077896 | tf_op jit(solution)/shard_map/ppermute | solution.py:630
  191.6 20.3 %collective-permute-start.31 = (bf16[1536,768]{1,0:T(8,128)(2,1)S(1)}, bf16[1536,768]{1,0:T(8,128)(2,1)S(1)}, u32[]{:S(2)}, u32[]{:S(2)}) collective-permute-start(bf16[1536,768]{1,0:T(8,128)(2,1)S(1)} %convolution_convert_fusion), channel_id=1, source_target_pairs={{0,4},{4,0},{8,12},{12,8},{16,20},{20,16},{24,28},{28,24},{1,5},{5... | collective-permute-start | bytes 7077896 | tf_op jit(solution)/shard_map/ppermute | solution.py:630
  203.7 13.0 %collective-permute-start.30 = (bf16[256,768]{1,0:T(8,128)(2,1)S(1)}, bf16[256,768]{1,0:T(8,128)(2,1)S(1)}, u32[]{:S(2)}, u32[]{:S(2)}) collective-permute-start(bf16[256,768]{1,0:T(8,128)(2,1)S(1)} %get-tuple-element.256), channel_id=1, source_target_pairs={{1,0},{2,1},{3,2},{5,4},{6,5},{7,6},{9,8},{10,9},{11,10},{13,12},{... | collective-permute-start | bytes 1179656 | tf_op jit(solution)/shard_map/ppermute | solution.py:602
  214.2 27.6 %collective-permute-start.33 = (bf16[2,4,96,768]{3,2,1,0:T(8,128)(2,1)S(1)}, bf16[2,4,96,768]{3,2,1,0:T(8,128)(2,1)S(1)}, u32[]{:S(2)}, u32[]{:S(2)}) collective-permute-start(bf16[2,4,96,768]{3,2,1,0:T(8,128)(2,1)S(1)} %slice_bitcast_fusion.1), channel_id=1, source_target_pairs={{0,8},{4,12},{8,0},{12,4},{16,24},{20,28},{24,16},{28,20},{1,9},{5... | collective-permute-start | bytes 3538952 | tf_op jit(solution)/shard_map/ppermute | solution.py:630
  214.7 27.3 %collective-permute-start.32 = (bf16[2,4,96,768]{3,2,1,0:T(8,128)(2,1)S(1)}, bf16[2,4,96,768]{3,2,1,0:T(8,128)(2,1)S(1)}, u32[]{:S(2)}, u32[]{:S(2)}) collective-permute-start(bf16[2,4,96,768]{3,2,1,0:T(8,128)(2,1)S(1)} %bitcast.264), channel_id=1, source_target_pairs={{0,16},{4,20},{8,24},{12,28},{16,0},{20,4},{24,8},{28,12},{1,17},{... | collective-permute-start | bytes 3538952 | tf_op jit(solution)/shard_map/ppermute | solution.py:630
  217.1 33.3 %collective-permute-start.35 = (bf16[2,4,32,768]{3,2,1,0:T(8,128)(2,1)S(1)}, bf16[2,4,32,768]{3,2,1,0:T(8,128)(2,1)S(1)}, u32[]{:S(2)}, u32[]{:S(2)}) collective-permute-start(bf16[2,4,32,768]{3,2,1,0:T(8,128)(2,1)S(1)} %bitcast.265), channel_id=1, source_target_pairs={{0,16},{4,20},{8,24},{12,28},{16,0},{20,4},{24,8},{28,12},{1,17},{... | collective-permute-start | bytes 1179656 | tf_op jit(solution)/shard_map/ppermute | solution.py:630
  251.1 18.0 %collective-permute-start.36 = (bf16[4,96,768]{2,1,0:T(8,128)(2,1)S(1)}, bf16[4,96,768]{2,1,0:T(8,128)(2,1)S(1)}, u32[]{:S(2)}, u32[]{:S(2)}) collective-permute-start(bf16[4,96,768]{2,1,0:T(8,128)(2,1)S(1)} %get-tuple-element.254), channel_id=1, source_target_pairs={{0,8},{4,12},{8,0},{12,4},{16,24},{20,28},{24,16},{28,20},{1,9},{5... | collective-permute-start | bytes 1769480 | tf_op jit(solution)/shard_map/ppermute | solution.py:630
  252.4 16.6 %collective-permute-start.37 = (bf16[4,96,768]{2,1,0:T(8,128)(2,1)S(1)}, bf16[4,96,768]{2,1,0:T(8,128)(2,1)S(1)}, u32[]{:S(2)}, u32[]{:S(2)}) collective-permute-start(bf16[4,96,768]{2,1,0:T(8,128)(2,1)S(1)} %get-tuple-element.252), channel_id=1, source_target_pairs={{0,16},{4,20},{8,24},{12,28},{16,0},{20,4},{24,8},{28,12},{1,17},{... | collective-permute-start | bytes 1769480 | tf_op jit(solution)/shard_map/ppermute | solution.py:630
  253.4 15.7 %collective-permute-start.38 = (bf16[4,32,768]{2,1,0:T(8,128)(2,1)S(1)}, bf16[4,32,768]{2,1,0:T(8,128)(2,1)S(1)}, u32[]{:S(2)}, u32[]{:S(2)}) collective-permute-start(bf16[4,32,768]{2,1,0:T(8,128)(2,1)S(1)} %get-tuple-element.280), channel_id=1, source_target_pairs={{0,8},{4,12},{8,0},{12,4},{16,24},{20,28},{24,16},{28,20},{1,9},{5... | collective-permute-start | bytes 589832 | tf_op jit(solution)/shard_map/ppermute | solution.py:630
  276.6 17.1 %collective-permute-start.52 = (bf16[2,224,768]{2,1,0:T(8,128)(2,1)S(1)}, bf16[2,224,768]{2,1,0:T(8,128)(2,1)S(1)}, u32[]{:S(2)}, u32[]{:S(2)}) collective-permute-start(bf16[2,224,768]{2,1,0:T(8,128)(2,1)S(1)} %pad_maximum_fusion.8), channel_id=1, source_target_pairs={{0,1},{1,0},{2,3},{3,2},{4,5},{5,4},{6,7},{7,6},{8,9},{9,8},{10,11... | collective-permute-start | bytes 2064392 | tf_op jit(solution)/shard_map/ppermute | solution.py:596
  280.7 13.0 %collective-permute-start.43 = (bf16[2,2,80,768]{3,2,1,0:T(8,128)(2,1)S(1)}, bf16[2,2,80,768]{3,2,1,0:T(8,128)(2,1)S(1)}, u32[]{:S(2)}, u32[]{:S(2)}) collective-permute-start(bf16[2,2,80,768]{3,2,1,0:T(8,128)(2,1)S(1)} %slice_bitcast_fusion.6), channel_id=1, source_target_pairs={{0,8},{4,12},{8,0},{12,4},{16,24},{20,28},{24,16},{28,20},{1,9},{5... | collective-permute-start | bytes 1474568 | tf_op jit(solution)/shard_map/ppermute | solution.py:630
  296.1 23.5 %collective-permute-start.53 = (bf16[224,768]{1,0:T(8,128)(2,1)S(1)}, bf16[224,768]{1,0:T(8,128)(2,1)S(1)}, u32[]{:S(2)}, u32[]{:S(2)}) collective-permute-start(bf16[224,768]{1,0:T(8,128)(2,1)S(1)} %fusion.39), channel_id=1, source_target_pairs={{0,2},{1,3},{2,0},{3,1},{4,6},{5,7},{6,4},{7,5},{8,10},{9,11},{10,... | collective-permute-start | bytes 1032200 | tf_op jit(solution)/shard_map/ppermute | solution.py:596
  300.5 21.8 %collective-permute-start.45 = (bf16[80,768]{1,0:T(8,128)(2,1)S(1)}, bf16[80,768]{1,0:T(8,128)(2,1)S(1)}, u32[]{:S(2)}, u32[]{:S(2)}) collective-permute-start(bf16[80,768]{1,0:T(8,128)(2,1)S(1)} %get-tuple-element.300), channel_id=1, source_target_pairs={{0,2},{1,3},{2,0},{3,1},{4,6},{5,7},{6,4},{7,5},{8,10},{9,11},{10,... | collective-permute-start | bytes 368648 | tf_op jit(solution)/shard_map/ppermute | solution.py:596
  302.0 20.3 %collective-permute-start.46 = (bf16[80,768]{1,0:T(8,128)(2,1)S(1)}, bf16[80,768]{1,0:T(8,128)(2,1)S(1)}, u32[]{:S(2)}, u32[]{:S(2)}) collective-permute-start(bf16[80,768]{1,0:T(8,128)(2,1)S(1)} %get-tuple-element.301), channel_id=1, source_target_pairs={{0,3},{1,2},{2,1},{3,0},{4,7},{5,6},{6,5},{7,4},{8,11},{9,10},{10,... | collective-permute-start | bytes 368648 | tf_op jit(solution)/shard_map/ppermute | solution.py:596
  303.2 19.1 %collective-permute-start.42 = (bf16[80,768]{1,0:T(8,128)(2,1)S(1)}, bf16[80,768]{1,0:T(8,128)(2,1)S(1)}, u32[]{:S(2)}, u32[]{:S(2)}) collective-permute-start(bf16[80,768]{1,0:T(8,128)(2,1)S(1)} %slice_bitcast_fusion.20), channel_id=1, source_target_pairs={{0,1},{1,0},{2,3},{3,2},{4,5},{5,4},{6,7},{7,6},{8,9},{9,8},{10,11... | collective-permute-start | bytes 368648 | tf_op jit(solution)/shard_map/ppermute | solution.py:596
  332.7 15.9 %collective-permute-start.58 = (bf16[4,2,1,112,768]{4,3,2,1,0:T(8,128)(2,1)S(1)}, bf16[4,2,1,112,768]{4,3,2,1,0:T(8,128)(2,1)S(1)}, u32[]{:S(2)}, u32[]{:S(2)}) collective-permute-start(bf16[4,2,1,112,768]{4,3,2,1,0:T(8,128)(2,1)S(1)} %pad_maximum_fusion.4), channel_id=1, source_target_pairs={{0,4},{4,0},{8,12},{12,8},{16,20},{20,16},{24,28},{28,24},{1,5},{5... | collective-permute-start | bytes 4128776 | tf_op jit(solution)/shard_map/ppermute | solution.py:630
  (119 other events, 766.3 us)
